TPU v7x, 128 devices: a whole 4x4x4 slice. The times are simulated.
128 devices in a mesh: shard: 16 (over x, z_hi, core), tensor: 8 (over z_lo, y).
Axes of the slice: x: 4, y: 4, z: 4 (z_hi: 2, z_lo: 2; z = z_hi * 2 + z_lo), core: 2. Of those that a mesh axis runs over, the one named last changes fastest.
Arguments:
- hidden_in: bfloat16 [12288, 8192], P('shard'), may hold values from -720 to 720
- policy_weights: bfloat16 [2, 8192, 1024], P(None, 'shard', 'tensor'), may hold values from -6 to 6
- reference_weights: bfloat16 [2, 8192, 1024], P(None, None, 'tensor'), may hold values from -6 to 6
- policy_queries: bfloat16 [12288, 4096], P('shard', 'tensor'), may hold values from -180 to 180
- reference_queries: bfloat16 [12288, 4096], P('shard', 'tensor'), may hold values from -180 to 180
- readout: bfloat16 [12288, 4096], P('shard', 'tensor'), may hold values from -90 to 90
- lengths: int32 [32], P('shard'), may hold values from 96 to 384, as said below
Outputs:
- new_policy: bfloat16 [2, 8192, 1024], P(None, 'shard', 'tensor')
- new_reference: bfloat16 [2, 8192, 1024], P(None, None, 'tensor')
- margins: float32 [16], P('shard')
Inputs may be any that keep to these rules, and one draw needn't show every extreme that they name: The first lengths[s] positions of sequence s are real, the rest padding; some sequence has all 384 real.
All inputs are finite; a program needn't handle non-finite values.
Results may differ from a plain program's by a relative error of at most 0.0087.
Values may be sent and summed in bfloat16 or wider, within the bound.
A program may use at most 128 MiB of HBM per device.

v0:
```python
import math

import jax
import jax.numpy as jnp
from jax import lax
from jax.sharding import PartitionSpec as P

D = 8192
HD = 128
KVH = 8
QH = 32
LEN = 384


rope_base = 1000000.0
dpo_beta = 0.1
learning_rate = 0.2
mix_alpha = 0.6
norm_eps = 1e-06


def rope_tables(seq_count, seq_len, head_size):
    positions = jnp.tile(jnp.arange(seq_len, dtype=jnp.float32), seq_count)
    freq_index = jnp.arange(head_size // 2, dtype=jnp.float32)
    frequency = rope_base ** (-2.0 * freq_index / head_size)
    angles = positions[:, None] * frequency[None, :]
    return (jnp.cos(angles)[:, None, :], jnp.sin(angles)[:, None, :])


def rotate_half(vectors, cosine, sine_table):
    half_size = vectors.shape[-1] // 2
    first_half = vectors[..., :half_size]
    second_half = vectors[..., half_size:]
    return jnp.concatenate(
        [
            first_half * cosine - second_half * sine_table,
            second_half * cosine + first_half * sine_table,
        ],
        axis=-1,
    )


def rounded(values):
    return lax.optimization_barrier(values.astype(jnp.bfloat16)).astype(jnp.float32)


def masked_scores(key_rows, value_rows, queries, readout, lengths, seq_len, total_heads):
    seq_count = lengths.shape[0]
    kv_heads = key_rows.shape[1]
    head_size = key_rows.shape[2]
    groups = queries.shape[1] // (kv_heads * head_size)
    query_f = queries.reshape(seq_count, seq_len, kv_heads, groups, head_size).astype(jnp.float32)
    key_f = key_rows.reshape(seq_count, seq_len, kv_heads, head_size).astype(jnp.float32)
    value_f = value_rows.reshape(seq_count, seq_len, kv_heads, head_size).astype(jnp.float32)
    logits = jnp.einsum("sikgd,sjkd->skgij", query_f, key_f) / math.sqrt(head_size)
    positions = jnp.arange(seq_len)
    causal = positions[:, None] >= positions[None, :]
    live_keys = positions[None, :] < lengths[:, None]
    allowed = causal[None, None, None, :, :] & live_keys[:, None, None, None, :]
    logits = jnp.where(allowed, logits, -1e30)
    row_max = jnp.max(logits, axis=-1, keepdims=True)
    exponent = jnp.exp(logits - row_max)
    probability = rounded(exponent / jnp.sum(exponent, axis=-1, keepdims=True))
    attended = rounded(jnp.einsum("skgij,sjkd->sikgd", probability, value_f))
    readout_f = readout.reshape(seq_count, seq_len, kv_heads, groups, head_size).astype(jnp.float32)
    token_logit = jnp.sum(attended * readout_f, axis=(2, 3, 4)) / math.sqrt(total_heads * head_size)
    return jnp.sum(jnp.where(live_keys, token_logit, 0.0), axis=1)


def body(
    hidden_in,
    policy_weights,
    reference_weights,
    policy_queries,
    reference_queries,
    readout,
    lengths,
):
    token_count = hidden_in.shape[0]
    seq_count = lengths.shape[0]
    local_rows = policy_weights.shape[1]
    columns = reference_weights.shape[2]
    kv_local = columns // HD
    hidden_f = hidden_in.astype(jnp.float32)
    inverse = lax.rsqrt(jnp.mean(hidden_f * hidden_f, axis=-1, keepdims=True) + norm_eps)
    normed = (hidden_f * inverse).astype(jnp.bfloat16)
    cosine, sine_table = rope_tables(seq_count, LEN, HD)
    width_scale = D ** (-0.5)

    def split_heads(projected):
        key_rows = rotate_half(
            projected[:, 0].reshape(token_count, kv_local, HD), cosine, sine_table
        ).astype(jnp.bfloat16)
        value_rows = projected[:, 1].reshape(token_count, kv_local, HD).astype(jnp.bfloat16)
        return (key_rows, value_rows)

    ref_projected = jnp.einsum(
        "td,kdc->tkc", normed, reference_weights, preferred_element_type=jnp.float32
    )
    ref_keys, ref_values = split_heads(ref_projected * width_scale)
    reference_part = masked_scores(
        ref_keys, ref_values, reference_queries, readout, lengths, LEN, QH
    )
    block_cols = normed
    policy_projected = jnp.einsum(
        "tn,knc->tkc",
        block_cols,
        lax.all_gather(policy_weights, "shard", axis=1, tiled=True),
        preferred_element_type=jnp.float32,
    )
    pol_keys, pol_values = split_heads(policy_projected * width_scale)

    def policy_part(key_rows, value_rows):
        return masked_scores(key_rows, value_rows, policy_queries, readout, lengths, LEN, QH)

    policy_local, pullback = jax.vjp(policy_part, pol_keys, pol_values)
    reference_total, policy_total = lax.psum((reference_part, policy_local), "tensor")
    paired = (policy_total - reference_total).reshape(-1, 2)
    margins = dpo_beta * (paired[:, 0] - paired[:, 1])
    weight = jax.nn.sigmoid(-margins)
    coefficient = jnp.stack([-weight, weight], axis=1).reshape(-1)
    key_grad, value_grad = pullback(coefficient)
    key_pre = rotate_half(key_grad.astype(jnp.float32), cosine, -sine_table).astype(jnp.bfloat16)
    cotangent = jnp.concatenate(
        [key_pre.reshape(token_count, columns), value_grad.reshape(token_count, columns)], axis=1
    )
    contract = (((0,), (0,)), ((), ()))
    block_cols = normed
    own_rows = lax.psum_scatter(
        lax.dot_general(block_cols, cotangent, contract, preferred_element_type=jnp.float32).astype(
            jnp.bfloat16
        ),
        "shard",
        scatter_dimension=0,
        tiled=True,
    ).astype(jnp.float32)
    gradient = own_rows.reshape(local_rows, 2, columns).transpose(1, 0, 2)
    squares = lax.psum(jnp.sum(gradient * gradient, axis=(1, 2)), ("shard", "tensor"))
    scale_factor = lax.rsqrt(squares / (D * KVH * HD) + norm_eps)
    new_rows = (
        policy_weights.astype(jnp.float32) - learning_rate * scale_factor[:, None, None] * gradient
    ).astype(jnp.bfloat16)
    new_full = lax.all_gather(new_rows, "shard", axis=1, tiled=True)
    new_reference = (
        mix_alpha * new_full.astype(jnp.float32)
        + (1.0 - mix_alpha) * reference_weights.astype(jnp.float32)
    ).astype(jnp.bfloat16)
    return (new_rows, new_reference, margins)


def solution(mesh):
    return jax.shard_map(
        body,
        mesh=mesh,
        in_specs=(
            P("shard", None),
            P(None, "shard", "tensor"),
            P(None, None, "tensor"),
            P("shard", "tensor"),
            P("shard", "tensor"),
            P("shard", "tensor"),
            P("shard"),
        ),
        out_specs=(P(None, "shard", "tensor"), P(None, None, "tensor"), P("shard")),
        check_vma=False,
    )
```

profile of v0, /device:TPU:1, one launch (start us, length us, event | category | flops | bytes accessed | tf_op | source)
XLA Modules:
  0.0 367.2 jit_solution(8643791465809988369)
XLA Ops:
  7.2 1.9 copy.31
  9.2 6.4 %copy.38 = bf16[2,8192,128]{1,2,0:T(8,128)(2,1)} copy(bf16[2,8192,128]{2,1,0:T(8,128)(2,1)} %param.9) | data formatting | bytes 8388608 | tf_op args[2]
  15.6 1.1 reshape.438
  16.8 0.2 reshape.441
  17.0 0.5 reshape.450
  17.5 1.7 copy.37
  19.3 7.1 %fusion = f32[768]{0:T(1024)S(1)} fusion(bf16[768,8192]{1,0:T(8,128)(2,1)} %param.7), kind=kLoop, calls=%fused_computation.2 | loop fusion | flops 18873600 | bytes 12585984 | tf_op jit(solution)/shard_map/reduce_sum | solution.py:85
  26.4 0.2 broadcast_and_fusion
  26.6 10.3 %fusion.107 = f32[768,256]{0,1} fusion(bf16[8192,256]{0,1:T(8,128)(2,1)} %bitcast.168, bf16[768,8192]{1,0:T(8,128)(2,1)} %param.7, f32[768]{0:T(1024)S(1)} %add_rsqrt_fusion), kind=kOutput, calls=%fused_computation.129 | convolution fusion | flops 3240099840 | bytes 17566720
  37.0 36.7 %all-gather.3.cloned.1.call-done = bf16[2,8192,128]{1,2,0:T(8,128)(2,1)} async-done(((bf16[2,512,128]{1,2,0:T(8,128)(2,1)}), bf16[2,8192,128]{1,2,0:T(8,128)(2,1)}) %all-gather.3.cloned.1.call-update) | async-done | bytes 4194320 | tf_op jit(solution)/shard_map/all_gather | solution.py:108
  73.7 9.4 %fusion.109 = f32[768,256]{0,1:S(1)} fusion(bf16[8192,256]{0,1:T(8,128)(2,1)} %bitcast.182, bf16[768,8192]{1,0:T(8,128)(2,1)} %param.7, f32[768]{0:T(1024)S(1)} %add_rsqrt_fusion), kind=kOutput, calls=%fused_computation.130 | convolution fusion | flops 3240099840 | bytes 17566720
  83.2 0.7 slice.66
  83.9 1.5 fusion.85
  85.4 0.2 copy.69
  85.6 1.1 copy.70
  86.7 0.2 copy.73
  86.8 0.2 copy.74
  87.0 0.8 fusion.57
  87.9 2.0 fusion.15
  89.8 2.0 fusion.12
  91.9 3.3 divide_convert_fusion.1
  95.2 0.2 copy.62
  95.4 1.6 fusion.35
  97.1 2.2 fusion.32
  99.3 2.0 multiply_reduce_fusion
  101.3 0.2 select_reduce_fusion
  101.5 15.0 %all-reduce = (f32[2]{0:T(128)S(1)}, f32[2]{0:T(128)S(1)}) all-reduce(f32[2]{0:T(128)S(1)} %get-tuple-element.10, f32[2]{0:T(128)S(1)} %get-tuple-element.9), channel_id=1, replica_groups=mesh['shard'=16,'tensor'=8] {'tensor'}, use_global_device_ids=true, to_apply=%region_5.6 | all-reduce | flops 4 | bytes 32 | tf_op jit(solution)/shard_map/psum | solution.py:117
  116.5 0.6 fusion.113
  118.6 2.8 multiply_convert_fusion
  121.5 2.3 copy.50
  123.7 1.9 convert_bitcast_fusion
  125.6 2.1 fusion.50
  127.8 3.9 %fusion.5 = f32[2,4,384]{2,1,0:T(4,128)S(1)} fusion(bf16[2,1,4,384,384]{3,4,2,0,1:T(8,128)(2,1)S(1)} %convert_bitcast_fusion, f32[2,4,384]{2,1,0:T(4,128)S(1)} %multiply_divide_fusion, f32[2,4,384]{2,1,0:T(4,128)S(1)} %get-tuple-element.8, f32[2,384,384,4]{2,1,3,0:T(8,128)} %copy-done, pred[2,384,384]{1,2,0:T(8,128)(4,1)S(1)} %broadcast_and_fusion), kind=kLoop, calls=%fused_computation.11 | loop fusion | flops 8254464 | bytes 7409664 | tf_op jit(solution)/shard_map/transpose(jvp())/reduce_sum | solution.py:63
  131.7 2.6 convert_reduce_fusion
  134.3 3.2 fusion.47
  137.6 0.2 fusion.112
  138.1 0.8 fusion.98
  138.9 0.2 copy.53
  139.1 0.2 copy.54
  139.2 0.2 copy.52
  139.4 11.1 %convolution_convert_fusion = bf16[8192,256]{1,0:T(8,128)(2,1)} fusion(bf16[768,128]{1,0:T(8,128)(2,1)S(1)} %bitcast.178, bf16[768,64]{1,0:T(8,128)(2,1)S(1)} %copy.54, bf16[768,64]{1,0:T(8,128)(2,1)S(1)} %copy.53, bf16[768,8192]{1,0:T(8,128)(2,1)} %param.7, f32[768]{0:T(1024)S(1)} %add_rsqrt_fusion), kind=kOutput, calls=%fused_computation.4 | convolution fusion | flops 3243376640 | bytes 17173504 | tf_op jit(solution)/shard_map/dot_general | solution.py:130
  150.6 79.4 %reduce-scatter.2.cloned.1.call-done = bf16[512,256]{1,0:T(8,128)(2,1)} async-done(((bf16[8192,256]{1,0:T(8,128)(2,1)}), bf16[512,256]{1,0:T(8,128)(2,1)}) %reduce-scatter.2.cloned.1.call-update) | async-done | bytes 262160 | tf_op jit(solution)/shard_map/reduce_scatter | solution.py:129
  230.0 1.2 reshape.453
  231.2 0.7 multiply_reduce_fusion.2
  231.8 65.7 %psum.23 = f32[2]{0:T(128)S(1)} all-reduce(f32[2]{0:T(128)S(1)} %multiply_reduce_fusion.2), channel_id=1, replica_groups=mesh['shard'=16,'tensor'=8] {'shard','tensor'}, use_global_device_ids=true, to_apply=%region_16.17 | all-reduce | flops 2 | bytes 16 | tf_op jit(solution)/shard_map/psum | solution.py:138
  297.6 1.8 fusion.61
  299.4 53.0 %all-gather.5.cloned.1.call-done = bf16[2,8192,128]{2,1,0:T(8,128)(2,1)} async-done(((bf16[2,512,128]{2,1,0:T(8,128)(2,1)}), bf16[2,8192,128]{2,1,0:T(8,128)(2,1)}) %all-gather.5.cloned.1.call-update) | async-done | bytes 4194320 | tf_op jit(solution)/shard_map/all_gather | solution.py:143
  352.5 7.1 %add_convert_fusion = bf16[2,8192,128]{2,1,0:T(8,128)(2,1)} fusion(bf16[2,8192,128]{2,1,0:T(8,128)(2,1)} %param.9, bf16[2,8192,128]{2,1,0:T(8,128)(2,1)} %all-gather.5.cloned.1.call-done), kind=kLoop, calls=%fused_computation.5 | loop fusion | flops 12582912 | bytes 12582912 | tf_op jit(solution)/shard_map/convert_element_type | solution.py:147
  (53 shorter events, 1.2 us)
Async XLA Ops:
  7.2 8.5 %copy-start.5 = (bf16[768,512]{1,0:T(8,128)(2,1)S(1)}, bf16[768,512]{1,0:T(8,128)(2,1)}, u32[]{:S(2)}) copy-start(bf16[768,512]{1,0:T(8,128)(2,1)} %param.10) | copy-start | bytes 2359300
  7.2 66.5 %all-gather.3.cloned.1.call-start = ((), (), s32[]{:S(2)}) async-start(), calls=%async_computation.1 | async-start | bytes 4456448 | tf_op jit(solution)/shard_map/all_gather | solution.py:108
  9.1 7.7 %copy-start.6 = (bf16[768,512]{1,0:T(8,128)(2,1)S(1)}, bf16[768,512]{1,0:T(8,128)(2,1)}, u32[]{:S(2)}) copy-start(bf16[768,512]{1,0:T(8,128)(2,1)} %param.11) | copy-start | bytes 2359300
  9.1 7.8 %copy-start.8 = (bf16[768,512]{1,0:T(8,128)(2,1)S(1)}, bf16[768,512]{1,0:T(8,128)(2,1)}, u32[]{:S(2)}) copy-start(bf16[768,512]{1,0:T(8,128)(2,1)} %param.12) | copy-start | bytes 2359300
  9.1 220.9 %reduce-scatter.2.cloned.1.call-start = ((), (), s32[]{:S(2)}) async-start(), calls=%async_computation.2 | async-start | bytes 4456448 | tf_op jit(solution)/shard_map/reduce_scatter | solution.py:129
  15.6 3.6 copy-start.10
  17.5 19.5 %copy-start.1 = (f32[2,384,1,4,128]{4,3,1,0,2:T(4,128)}, f32[2,384,1,4,128]{4,3,1,0,2:T(4,128)S(1)}, u32[]{:S(2)}) copy-start(f32[2,384,1,4,128]{4,3,1,0,2:T(4,128)S(1)} %reshape.450) | copy-start | bytes 4718596
  73.7 9.4 %copy-start.9 = (f32[768,256]{0,1:S(1)}, f32[768,256]{0,1}, u32[]{:S(2)}) copy-start(f32[768,256]{0,1} %fusion.107) | copy-start | bytes 2359300
  83.0 4.0 %copy-start.2 = (bf16[2,384,4,128]{3,2,1,0:T(4,128)(2,1)S(1)}, bf16[2,384,4,128]{3,2,1,0:T(4,128)(2,1)}, u32[]{:S(2)}) copy-start(bf16[2,384,4,128]{3,2,1,0:T(4,128)(2,1)} %reshape.438) | copy-start | bytes 2359300
  87.8 4.0 %copy-start = (f32[2,384,384,4]{2,1,3,0:T(8,128)}, f32[2,384,384,4]{2,1,3,0:T(8,128)S(1)}, u32[]{:S(2)}) copy-start(f32[2,384,384,4]{2,1,3,0:T(8,128)S(1)} %fusion.57) | copy-start | bytes 14155780
  91.9 5.2 %copy-start.7 = (bf16[768,1,128]{0,2,1:T(8,128)(2,1)S(1)}, bf16[768,1,128]{0,2,1:T(8,128)(2,1)}, u32[]{:S(2)}) copy-start(bf16[768,1,128]{0,2,1:T(8,128)(2,1)} %slice.66) | copy-start | bytes 589828
  121.5 10.2 %slice-start = ((s8[4718592]{0:T(1024)(128)(4,1)}), s8[524288]{0:T(1024)(128)(4,1)S(1)}, s32[]{:S(2)}) async-start(s8[4718592]{0:T(1024)(128)(4,1)} %bitcast.166), calls=%async_computation.4 | async-start | bytes 1048576
  125.6 6.0 %slice-start.1 = ((s8[4718592]{0:T(1024)(128)(4,1)}), s8[4194304]{0:T(1024)(128)(4,1)S(1)}, s32[]{:S(2)}) async-start(s8[4718592]{0:T(1024)(128)(4,1)} %bitcast.166), calls=%async_computation.5 | async-start | bytes 8388608
  131.6 2.7 copy-start.3
  150.6 147.0 %copy-start.4 = (bf16[2,512,128]{2,1,0:T(8,128)(2,1)S(1)}, bf16[2,512,128]{2,1,0:T(8,128)(2,1)}, u32[]{:S(2)}) copy-start(bf16[2,512,128]{2,1,0:T(8,128)(2,1)} %param.8) | copy-start | bytes 786436
  150.6 201.9 %all-gather.5.cloned.1.call-start = ((), (), s32[]{:S(2)}) async-start(), calls=%async_computation.3 | async-start | bytes 4456448 | tf_op jit(solution)/shard_map/all_gather | solution.py:143
Sparse Core Ops, SparseCore 0:
  10.8 62.7 all-gather.2
  150.7 79.2 reduce-scatter.1
  299.6 52.8 all-gather.4
where the time goes:
time: 368 us; the launch traced here: 367 us
  waiting for transfers between devices  169 us (46%)
  blocking collectives  80.8 us (22%)
  matrix products  44.6 us (12%)
  other arithmetic  36.5 us (10%)
  local copies, waits for them, and re-layouts  19.4 us (5%)
  between operations  16.6 us (5%)
    reduce_scatter x1, waiting for transfers between devices, body(): lax.psum_scatter(lax.dot_general(block_cols, cotangent, contract, preferr...  79.4 us
    psum x1, blocking collectives, body(): lax.psum(jnp.sum(gradient * gradient, axis=(1, 2)), ('shard', 'tensor'))  65.7 us
    all_gather x1, waiting for transfers between devices, body(): new_full = lax.all_gather(new_rows, 'shard', axis=1, tiled=True)  53 us
    all_gather x1, waiting for transfers between devices, body(): lax.all_gather(policy_weights, 'shard', axis=1, tiled=True)  36.7 us
    unnamed x2, matrix products  19.7 us
    psum x1, blocking collectives, body(): lax.psum((reference_part, policy_local), 'tensor')  15 us
    dot_general x1, matrix products, body(): lax.dot_general(block_cols, cotangent, contract, preferred_element_type=j...  11.1 us
    unnamed x30, local copies, waits for them, and re-layouts  8.64 us
  transfers between devices with their start and end apart: 3, of which 3 were waited for; matrix products, arithmetic and copies ran while one was open for 8% of the time, Pallas kernels for 0%

commit v1 on v0

v1 whole, which is shorter than its diff:
```python
import math

import jax
import jax.numpy as jnp
import numpy as np
from jax import lax
from jax.experimental import pallas as pl
from jax.experimental.pallas import tpu as pltpu
from jax.sharding import PartitionSpec as P

D = 8192
HD = 128
KVH = 8
QH = 32
LEN = 384
TOK = 2 * LEN
HEADS = 4
NS = 16
NT = 8
ROWS = D // NS
QB = 128
NB = LEN // QB

rope_base = 1000000.0
dpo_beta = 0.1
learning_rate = 0.2
mix_alpha = 0.6
norm_eps = 1e-06

MESH = pl.DeviceIdType.MESH
BF = jnp.bfloat16
F32 = jnp.float32

OWN, LFT, RGT, ZED, OPP, ZLF, ZRG, ZOP = range(8)


def rope_constants():
    positions = np.arange(LEN, dtype=np.float32)
    index = np.arange(HD // 2, dtype=np.float32)
    frequency = (np.float32(rope_base) ** (np.float32(-2.0) * index / np.float32(HD))).astype(np.float32)
    angles = (positions[:, None] * frequency[None, :]).astype(np.float32)
    cosine, sine = np.cos(angles), np.sin(angles)
    wide_cos = np.concatenate([cosine, cosine], axis=1)
    wide_sin = np.concatenate([-sine, sine], axis=1)
    return np.stack([wide_cos, wide_sin]), np.stack([wide_cos.T[: HD // 2], sine.T])


def dot(a, b, contract=((1,), (0,))):
    return lax.dot_general(a, b, (contract, ((), ())), preferred_element_type=F32)


def kernel(
    hid, pw, rw, pq, rq, ro, lens, rope, rope_t,
    newp, newr, marg,
    normed, pfull, gfull, rwv, pqv, rqv, rov, ropev, ropetv,
    acc, keys, values, cot, probs, grad_t,
    partial, sib_send, sib_recv, stage, net_recv,
    score_buf, sq_tensor, sq_shard, newp_v,
    hid_sem, load_sem, store_sem,
    g1_send, g1_recv, s1_send, s1_recv,
    g2_send, g2_recv, s2_send, s2_recv,
    rs_sib_send, rs_sib_recv, rs_send, rs_recv,
    sc_send, sc_recv, qt_send, qt_recv, qs_send, qs_recv,
):
    s = lax.axis_index("shard")
    t = lax.axis_index("tensor")
    x, h, c = s // 4, (s // 2) % 2, s % 2

    def shard_of(xx, hh, cc):
        return lax.rem(xx, 4) * 4 + hh * 2 + cc

    left = (shard_of(x + 3, h, c), t)
    right = (shard_of(x + 1, h, c), t)
    zed = (shard_of(x, 1 - h, c), t)
    sib = (shard_of(x, h, 1 - c), t)

    pair = {
        OWN: (x, h),
        LFT: (x + 3, h),
        RGT: (x + 1, h),
        ZED: (x, 1 - h),
        OPP: (x + 2, h),
        ZLF: (x + 3, 1 - h),
        ZRG: (x + 1, 1 - h),
        ZOP: (x + 2, 1 - h),
    }

    def rows_of(pos, cc):
        return pl.ds(pl.multiple_of(shard_of(*pair[pos], cc) * ROWS, ROWS), ROWS)

    def pair_rows(pos):
        return pl.ds(pl.multiple_of(shard_of(*pair[pos], 0) * ROWS, 2 * ROWS), 2 * ROWS)

    pending = []

    def send(src, dst, send_sem, recv_sem, device):
        copy = pltpu.make_async_remote_copy(
            src_ref=src, dst_ref=dst, send_sem=send_sem, recv_sem=recv_sem,
            device_id=device, device_id_type=MESH,
        )
        copy.start()
        pending.append(copy)

    def arrived(dst, recv_sem, send_sem, device):
        pltpu.make_async_remote_copy(
            src_ref=dst, dst_ref=dst, send_sem=send_sem, recv_sem=recv_sem,
            device_id=device, device_id_type=MESH,
        ).wait_recv()

    loads = []

    def load(src, dst, i):
        copy = pltpu.make_async_copy(src, dst, load_sem.at[i])
        copy.start()
        loads.append(copy)

    hid_copies = []
    for b in range(3):
        copy = pltpu.make_async_copy(hid.at[pl.ds(256 * b, 256)], normed.at[pl.ds(256 * b, 256)], hid_sem.at[b])
        copy.start()
        hid_copies.append(copy)
        if b == 0:
            load(rw, rwv, 0)
    load(rq, rqv, 1)
    load(ro, rov, 2)
    load(rope, ropev, 3)
    load(pq, pqv, 4)
    load(rope_t, ropetv, 5)
    own_rows = rows_of(OWN, c)
    load(pw, pfull.at[:, own_rows, :], 6)

    barrier = pltpu.get_barrier_semaphore()
    for r in range(1, NS):
        pl.semaphore_signal(barrier, inc=1, device_id=(lax.rem(s + r, NS), t), device_id_type=MESH)
    for r in range(1, NT):
        pl.semaphore_signal(barrier, inc=1, device_id=(s, lax.rem(t + r, NT)), device_id_type=MESH)
    pl.semaphore_wait(barrier, NS + NT - 2)

    class Gather:
        def __init__(self, buf, own, send_sem, recv_sem, sib_send_sem, sib_recv_sem):
            self.buf, self.own = buf, own
            self.send_sem, self.recv_sem = send_sem, recv_sem
            self.sib_send_sem, self.sib_recv_sem = sib_send_sem, sib_recv_sem
            self.count = 0

        def block(self, pos, cc, k):
            return self.buf.at[k, rows_of(pos, cc), :]

        def to(self, src, dst_pos_here, k, arrive_as, device):
            send(src, self.block(dst_pos_here, c, k), self.send_sem.at[self.count],
                 self.recv_sem.at[arrive_as, k], device)
            self.count += 1

        def to_sib(self, src, pos, k):
            send(src, self.block(pos, c, k), self.sib_send_sem.at[pos, k], self.sib_recv_sem.at[pos, k], sib)

        def start(self, k):
            src = self.own(k)
            self.to(src, OWN, k, LFT, right)
            self.to(src, OWN, k, RGT, left)
            self.to(src, OWN, k, ZED, zed)
            self.to_sib(src, OWN, k)

        def take(self, pos, k, device):
            arrived(self.block(pos, c, k), self.recv_sem.at[pos, k], self.send_sem.at[0], device)
            src = self.block(pos, c, k)
            if pos == LFT and k == 0:
                self.to(src, pos, k, OPP, right)
            if pos == RGT and k == 1:
                self.to(src, pos, k, OPP, left)
            if pos == ZED:
                self.to(src, pos, k, ZLF, right)
                self.to(src, pos, k, ZRG, left)
            if pos == OPP:
                self.to(src, pos, k, ZOP, zed)
            self.to_sib(src, pos, k)

        def event(self, i):
            if i == 0:
                self.take(LFT, 0, left)
                self.take(RGT, 1, right)
                self.take(ZED, 0, zed)
            elif i == 1:
                self.take(LFT, 1, left)
                self.take(RGT, 0, right)
                self.take(ZED, 1, zed)
            elif i == 2:
                self.take(OPP, 0, left)
                self.take(OPP, 1, right)
            else:
                self.take(ZLF, i - 3, left)
                self.take(ZRG, i - 3, right)
                self.take(ZOP, i - 3, zed)

        def from_sib(self, pos):
            for k in range(2):
                arrived(self.block(pos, 1 - c, k), self.sib_recv_sem.at[pos, k], self.sib_send_sem.at[pos, k], sib)

    g1 = Gather(pfull, lambda k: pw.at[k], g1_send, g1_recv, s1_send, s1_recv)
    g1.start(0)
    g1.start(1)

    def normalise(b):
        hid_copies[b].wait()

        @pl.loop(0, 8)
        def _(i):
            rows = pl.ds(pl.multiple_of(256 * b + i * 32, 32), 32)
            total = jnp.zeros((32, 512), F32)
            for j in range(D // 512):
                part = normed[rows, pl.ds(512 * j, 512)].astype(F32)
                total = total + part * part
            inverse = lax.rsqrt(jnp.sum(total, axis=-1, keepdims=True) * (1.0 / D) + norm_eps)
            for j in range(D // 512):
                cols = pl.ds(512 * j, 512)
                normed[rows, cols] = (normed[rows, cols].astype(F32) * inverse).astype(BF)

    def project(rows, weights, cols, first):
        both = jnp.concatenate([weights[0, cols, :], weights[1, cols, :]], axis=1)
        product = dot(normed[rows, cols], both)
        acc[rows, :] = product if first else acc[rows, :] + product

    def project_reference(b):
        rows = pl.ds(256 * b, 256)
        acc[rows, :] = jnp.zeros((256, 2 * HD), F32)

        @pl.loop(0, 8)
        def _(j):
            project(rows, rwv, pl.ds(pl.multiple_of(j * 1024, 1024), 1024), False)

    def heads_out(which):
        for q in range(2):
            rows = pl.ds(LEN * q, LEN)
            raw = acc[rows, 0:HD] * (D ** -0.5)
            turned = raw * ropev[0] + pltpu.roll(raw, HD // 2, 1) * ropev[1]
            keys[rows, :] = turned.astype(BF)
            values[rows, :] = (acc[rows, HD:] * (D ** -0.5)).astype(BF)

    def stacked(ref, q, b):
        rows = pl.ds(LEN * q + QB * b, QB)
        return jnp.concatenate([ref[rows, pl.ds(HD * g, HD)] for g in range(HEADS)], axis=0)

    def attend(q, b, queries, keep):
        n = QB * (b + 1)
        live = lens[q]
        seen = pl.ds(LEN * q, n)
        logits = dot(stacked(queries, q, b), keys[seen, :], ((1,), (1,))) * (1.0 / math.sqrt(HD))
        row = lax.broadcasted_iota(jnp.int32, (HEADS * QB, n), 0)
        at = QB * b + lax.rem(row, QB)
        key_at = lax.broadcasted_iota(jnp.int32, (HEADS * QB, n), 1)
        allowed = jnp.logical_and(key_at <= at, key_at < live)
        logits = jnp.where(allowed, logits, -1e30)
        exponent = jnp.exp(logits - jnp.max(logits, axis=-1, keepdims=True))
        probability = exponent / jnp.sum(exponent, axis=-1, keepdims=True)
        if keep:
            probs[q, b, :, 0:n] = probability
        attended = dot(probability.astype(BF), values[seen, :]).astype(BF).astype(F32)
        product = attended * stacked(rov, q, b).astype(F32)
        real = QB * b + lax.rem(lax.broadcasted_iota(jnp.int32, product.shape, 0), QB) < live
        product = jnp.where(real, product, 0.0)
        return jnp.sum(product.reshape(HEADS * QB // 8, 8, HD), axis=0)

    def scores(queries, keep):
        chosen = jnp.zeros((8, HD), F32)
        rejected = jnp.zeros((8, HD), F32)
        for b in range(NB):
            chosen = chosen + attend(0, b, queries, keep)
            rejected = rejected + attend(1, b, queries, keep)
        return chosen - rejected

    loads[0].wait()
    for b in range(3):
        normalise(b)
        project_reference(b)
        g1.event(b)
    for i in (1, 2, 3):
        loads[i].wait()
    heads_out(rqv)
    score_buf[t] = -scores(rqv, False)

    everyone = pl.ds(0, TOK)

    def project_policy(pos, first=False):
        g1.from_sib(pos)
        project(everyone, pfull, pair_rows(pos), first)

    loads[6].wait()
    loads[4].wait()
    loads[5].wait()
    project_policy(OWN, True)
    g1.event(3)
    for pos in (LFT, RGT, ZED, OPP):
        project_policy(pos)
    g1.event(4)
    for pos in (ZLF, ZRG, ZOP):
        project_policy(pos)

    heads_out(pqv)
    score_buf[t] = score_buf[t] + scores(pqv, True)
    for r in range(1, NT):
        send(score_buf.at[t], score_buf.at[t], sc_send.at[r], sc_recv.at[t], (s, lax.rem(t + r, NT)))

    def pull(q, b):
        n = QB * (b + 1)
        live = lens[q]
        seen = pl.ds(LEN * q, n)
        sign = -1.0 if q == 0 else 1.0
        out_cot = stacked(rov, q, b).astype(F32) * (sign / math.sqrt(QH * HD))
        real = QB * b + lax.rem(lax.broadcasted_iota(jnp.int32, out_cot.shape, 0), QB) < live
        out_cot = jnp.where(real, out_cot, 0.0).astype(BF)
        probability = probs[q, b, :, 0:n]
        prob_cot = dot(out_cot, values[seen, :], ((1,), (1,))).astype(BF).astype(F32)
        weighted = probability * prob_cot
        logit_cot = weighted - probability * jnp.sum(weighted, axis=-1, keepdims=True)
        value_t = dot(out_cot, probability.astype(BF), ((0,), (0,)))
        key_t = dot(stacked(pqv, q, b), logit_cot.astype(BF), ((0,), (0,)))
        if b == NB - 1:
            grad_t[0, :, seen] = key_t
            grad_t[1, :, seen] = value_t
        else:
            grad_t[0, :, seen] += key_t
            grad_t[1, :, seen] += value_t

    for q in range(2):
        for b in reversed(range(NB)):
            pull(q, b)
        tokens = pl.ds(LEN * q, LEN)
        key_grad = (grad_t[0, :, tokens] * (1.0 / math.sqrt(HD))).astype(BF).astype(F32)
        upper, lower = key_grad[: HD // 2], key_grad[HD // 2 :]
        cosine, sine = ropetv[0], ropetv[1]
        cot[0 : HD // 2, tokens] = (upper * cosine + lower * sine).astype(BF)
        cot[HD // 2 : HD, tokens] = (lower * cosine - upper * sine).astype(BF)
        cot[HD:, tokens] = grad_t[1, :, tokens].astype(BF)

    for r in range(1, NT):
        peer = lax.rem(t + r, NT)
        arrived(score_buf.at[peer], sc_recv.at[peer], sc_send.at[r], (s, peer))
    score_total = score_buf[0]
    for r in range(1, NT):
        score_total = score_total + score_buf[r]
    score_total = jnp.sum(jnp.sum(score_total, axis=1, keepdims=True), axis=0, keepdims=True)
    margin = score_total * (dpo_beta / math.sqrt(QH * HD))
    marg[...] = jnp.broadcast_to(margin, (8, HD))
    weight = 1.0 / (1.0 + jnp.exp(margin))

    def product_of(pos, cc):
        out = dot(cot[...], normed[:, rows_of(pos, cc)]) * weight
        return out[:HD].T, out[HD:].T

    order = (ZOP, ZRG, ZLF, OPP, ZED, RGT, LFT, OWN)
    sends = [0]

    def push(i, k, slot, device):
        send(stage.at[i, k], net_recv.at[slot, k], rs_send.at[sends[0]], rs_recv.at[slot, k], device)
        sends[0] += 1

    def pull_net(slot, k, device):
        arrived(net_recv.at[slot, k], rs_recv.at[slot, k], rs_send.at[0], device)
        return net_recv[slot, k].astype(F32)

    SLOT_Z1, SLOT_R2L, SLOT_R2R, SLOT_3, SLOT_Z4, SLOT_5L, SLOT_5R = range(7)

    def compute(i):
        for k, block in enumerate(product_of(order[i], 1 - c)):
            sib_send[i, k] = block.astype(BF)
        send(sib_send.at[i], sib_recv.at[i], rs_sib_send.at[i], rs_sib_recv.at[i], sib)
        for k, block in enumerate(product_of(order[i], c)):
            partial[i, k] = block

    def settle(i):
        arrived(sib_recv.at[i], rs_sib_recv.at[i], rs_sib_send.at[i], sib)

    def put(i, k, terms):
        total = partial[i, k] + sib_recv[i, k].astype(F32)
        for term in terms:
            total = total + term
        stage[i, k] = total.astype(BF)

    compute(0)
    compute(1)
    settle(0)
    for k in range(2):
        put(0, k, ())
        push(0, k, SLOT_Z1, zed)
    compute(2)
    settle(1)
    for k in range(2):
        put(1, k, ())
        push(1, k, SLOT_R2L, right)
    compute(3)
    settle(2)
    for k in range(2):
        put(2, k, ())
        push(2, k, SLOT_R2R, left)
    for i in range(4, 8):
        compute(i)
    for i in range(3, 8):
        settle(i)
    put(3, 0, (pull_net(SLOT_Z1, 0, zed),))
    push(3, 0, SLOT_3, right)
    put(3, 1, (pull_net(SLOT_Z1, 1, zed),))
    push(3, 1, SLOT_3, left)
    put(5, 1, ())
    push(5, 1, SLOT_5L, right)
    put(6, 0, ())
    push(6, 0, SLOT_5R, left)
    for k in range(2):
        put(4, k, (pull_net(SLOT_R2L, k, left), pull_net(SLOT_R2R, k, right)))
        push(4, k, SLOT_Z4, zed)
    put(5, 0, (pull_net(SLOT_3, 0, left),))
    push(5, 0, SLOT_5L, right)
    put(6, 1, (pull_net(SLOT_3, 1, right),))
    push(6, 1, SLOT_5R, left)

    g2 = Gather(gfull, lambda k: gfull.at[k, own_rows, :], g2_send, g2_recv, s2_send, s2_recv)
    for k in range(2):
        total = partial[7, k] + sib_recv[7, k].astype(F32)
        total = total + pull_net(SLOT_Z4, k, zed)
        total = total + pull_net(SLOT_5L, k, left)
        total = total + pull_net(SLOT_5R, k, right)
        gfull[k, own_rows, :] = total.astype(BF)
        g2.start(k)
        sq_tensor[t, k] = jnp.sum((total * total).reshape(ROWS // 8, 8, HD), axis=0)

    for r in range(1, NT):
        send(sq_tensor.at[t], sq_tensor.at[t], qt_send.at[r], qt_recv.at[t], (s, lax.rem(t + r, NT)))
    for r in range(1, NT):
        peer = lax.rem(t + r, NT)
        arrived(sq_tensor.at[peer], qt_recv.at[peer], qt_send.at[r], (s, peer))
    squares = sq_tensor[0]
    for r in range(1, NT):
        squares = squares + sq_tensor[r]
    sq_shard[s] = squares
    for r in range(1, NS):
        send(sq_shard.at[s], sq_shard.at[s], qs_send.at[r], qs_recv.at[s], (lax.rem(s + r, NS), t))
    g2.event(0)
    for r in range(1, NS):
        peer = lax.rem(s + r, NS)
        arrived(sq_shard.at[peer], qs_recv.at[peer], qs_send.at[r], (peer, t))
    squares = sq_shard[0]
    for r in range(1, NS):
        squares = squares + sq_shard[r]
    step = []
    for k in range(2):
        mean = jnp.sum(jnp.sum(squares[k], axis=1, keepdims=True), axis=0, keepdims=True) * (1.0 / (D * KVH * HD))
        step.append(learning_rate * lax.rsqrt(mean + norm_eps))

    stores = []

    def store(src, dst, i):
        copy = pltpu.make_async_copy(src, dst, store_sem.at[i])
        copy.start()
        stores.append(copy)

    def update(pos):
        g2.from_sib(pos)
        base = shard_of(*pair[pos], 0) * ROWS
        for k in range(2):

            @pl.loop(0, 8)
            def _(i):
                rows = pl.ds(pl.multiple_of(base + i * 128, 128), 128)
                fresh = (pfull[k, rows, :].astype(F32) - step[k] * gfull[k, rows, :].astype(F32)).astype(BF)
                if pos == OWN:
                    newp_v[k, pl.ds(pl.multiple_of(i * 128, 128), 128), :] = fresh
                mixed = mix_alpha * fresh.astype(F32) + (1.0 - mix_alpha) * rwv[k, rows, :].astype(F32)
                rwv[k, rows, :] = mixed.astype(BF)

            store(rwv.at[k, pair_rows(pos), :], newr.at[k, pair_rows(pos), :], 2 * pos + k)
        if pos == OWN:
            store(newp_v.at[:, pl.ds(pl.multiple_of(c * ROWS, ROWS), ROWS), :], newp, 16)

    g2.event(1)
    update(OWN)
    g2.event(2)
    for pos in (LFT, RGT, ZED):
        update(pos)
    g2.event(3)
    update(OPP)
    g2.event(4)
    for pos in (ZLF, ZRG, ZOP):
        update(pos)
    for copy in stores:
        copy.wait()
    for copy in pending:
        copy.wait_send()


def body(hidden_in, policy_weights, reference_weights, policy_queries, reference_queries, readout, lengths):
    rope, rope_t = rope_constants()
    anywhere = pl.BlockSpec(memory_space=pl.ANY)
    dma = pltpu.SemaphoreType.DMA
    block = (2, ROWS, HD)
    new_rows, new_reference, margins = pl.pallas_call(
        kernel,
        out_shape=(
            jax.ShapeDtypeStruct(block, BF),
            jax.ShapeDtypeStruct((2, D, HD), BF),
            jax.ShapeDtypeStruct((8, HD), F32),
        ),
        in_specs=[anywhere] * 6 + [pl.BlockSpec(memory_space=pltpu.SMEM)] + [anywhere] * 2,
        out_specs=(anywhere, anywhere, pl.BlockSpec(memory_space=pltpu.VMEM)),
        scratch_shapes=[
            pltpu.VMEM((TOK, D), BF),
            pltpu.VMEM((2, D, HD), BF),
            pltpu.VMEM((2, D, HD), BF),
            pltpu.VMEM((2, D, HD), BF),
            pltpu.VMEM((TOK, HEADS * HD), BF),
            pltpu.VMEM((TOK, HEADS * HD), BF),
            pltpu.VMEM((TOK, HEADS * HD), BF),
            pltpu.VMEM((2, LEN, HD), F32),
            pltpu.VMEM((2, HD // 2, LEN), F32),
            pltpu.VMEM((TOK, 2 * HD), F32),
            pltpu.VMEM((TOK, HD), BF),
            pltpu.VMEM((TOK, HD), BF),
            pltpu.VMEM((2 * HD, TOK), BF),
            pltpu.VMEM((2, NB, HEADS * QB, LEN), F32),
            pltpu.VMEM((2, HD, TOK), F32),
            pltpu.VMEM((8, *block), F32),
            pltpu.VMEM((8, *block), BF),
            pltpu.VMEM((8, *block), BF),
            pltpu.VMEM((8, *block), BF),
            pltpu.VMEM((7, *block), BF),
            pltpu.VMEM((NT, 8, HD), F32),
            pltpu.VMEM((NT, 2, 8, HD), F32),
            pltpu.VMEM((NS, 2, 8, HD), F32),
            pltpu.VMEM((2, 2 * ROWS, HD), BF),
            dma((3,)), dma((7,)), dma((17,)),
            dma((14,)), dma((8, 2)), dma((8, 2)), dma((8, 2)),
            dma((14,)), dma((8, 2)), dma((8, 2)), dma((8, 2)),
            dma((8,)), dma((8,)), dma((14,)), dma((7, 2)),
            dma((NT,)), dma((NT,)), dma((NT,)), dma((NT,)), dma((NS,)), dma((NS,)),
        ],
        compiler_params=pltpu.CompilerParams(
            collective_id=0, has_side_effects=True, vmem_limit_bytes=60 * 1024 * 1024
        ),
        cost_estimate=pl.CostEstimate(flops=12_000_000_000, bytes_accessed=24_000_000, transcendentals=2_000_000),
    )(
        hidden_in, policy_weights, reference_weights, policy_queries, reference_queries, readout, lengths,
        jnp.asarray(rope), jnp.asarray(rope_t),
    )
    return new_rows, new_reference, margins[0, :1]


def solution(mesh):
    return jax.shard_map(
        body,
        mesh=mesh,
        in_specs=(
            P("shard", None),
            P(None, "shard", "tensor"),
            P(None, None, "tensor"),
            P("shard", "tensor"),
            P("shard", "tensor"),
            P("shard", "tensor"),
            P("shard"),
        ),
        out_specs=(P(None, "shard", "tensor"), P(None, None, "tensor"), P("shard")),
        check_vma=False,
    )
```

time: 368 us -> 101 us (0.27)
  waiting for transfers between devices: 169 us -> 0 us
  Pallas kernels: 0 us -> 92.4 us
  blocking collectives: 80.8 us -> 0 us
  matrix products: 44.6 us -> 0 us
  other arithmetic: 36.5 us -> 0 us
  between operations: 16.6 us -> 0.64 us
  local copies, waits for them, and re-layouts: 19.4 us -> 7.33 us
    pallas_call x0 -> x1, Pallas kernels: none -> 92.4 us  [body(): pl.pallas_call(kernel, out_shape=(jax.ShapeDtypeStruct(block, BF), jax.Sh...]
    all_gather x2 -> x0, waiting for transfers between devices: 89.8 us -> none  [the longest x1 53 us: body(): new_full = lax.all_gather(new_rows, 'shard', axis=1, tiled=True)]
    psum x2 -> x0, blocking collectives: 80.8 us -> none  [the longest x1 65.7 us: body(): lax.psum(jnp.sum(gradient * gradient, axis=(1, 2)), ('shard', 'tensor'))]
    reduce_scatter x1 -> x0, waiting for transfers between devices: 79.4 us -> none  [body(): lax.psum_scatter(lax.dot_general(block_cols, cotangent, contract, preferr...]
    dot_general x8 -> x0, matrix products: 25 us -> none  [the longest x1 11.1 us: body(): lax.dot_general(block_cols, cotangent, contract, preferred_element_type=j...]
    unnamed x2 -> x0, matrix products: 19.7 us -> none
    reduce_sum x7 -> x0, other arithmetic: 18.4 us -> none  [the longest x1 7.14 us: body(): jnp.mean(hidden_f * hidden_f, axis=-1, keepdims=True) + norm_eps]
    convert_element_type x5 -> x0, other arithmetic: 15.1 us -> none  [the longest x1 7.1 us: body(): new_reference = (mix_alpha * new_full.astype(jnp.float32) + (1.0 - mix_al...]
  transfers between devices with their start and end apart: 3 -> 0, of which waited for: 3 -> 0; matrix products, arithmetic and copies ran while one was open for 8% -> 0% of each run, Pallas kernels for 0% -> 0%
where the time goes in v1:
time: 101 us; the launch traced here: 100 us
  Pallas kernels  92.4 us (91%)
  local copies, waits for them, and re-layouts  7.33 us (7%)
    pallas_call x1, Pallas kernels, body(): pl.pallas_call(kernel, out_shape=(jax.ShapeDtypeStruct(block, BF), jax.Sh...  92.4 us
    unnamed x2, local copies, waits for them, and re-layouts  6.14 us

profile of v1, /device:TPU:1, one launch (start us, length us, event | category | flops | bytes accessed | tf_op | source)
XLA Modules:
  0.0 100.4 jit_solution(4536968981825539590)
XLA Ops:
  0.6 92.4 %shard_map.112 = (bf16[2,512,128]{2,1,0:T(8,128)(2,1)}, bf16[2,8192,128]{2,1,0:T(8,128)(2,1)}, f32[8,128]{1,0:T(8,128)}) custom-call(bf16[768,8192]{1,0:T(8,128)(2,1)} %hid.1, bf16[2,512,128]{2,1,0:T(8,128)(2,1)} %pw.1, bf16[2,8192,128]{2,1,0:T(8,128)(2,1)} %rw.1, bf16[768,512]{1,0:T(8,128)(2,1)} %pq.1, bf16[768,512]{1,0:T(8,128)(2,1)} %rq.1, ...), custom_call_target="tpu_custom_call" | custom-call | flops 12000000000 | bytes 24000000 | tf_op jit(solution)/shard_map/pallas_call | solution.py:494
  93.1 1.2 %slice.3 = f32[1,1]{1,0:T(1,128)} slice(f32[8,128]{1,0:T(8,128)} %get-tuple-element.8), slice={[0:1], [0:1]} | slice | bytes 8 | tf_op jit(solution)/shard_map/slice | solution.py:542
  94.3 1.7 %copy.14 = bf16[2,512,128]{2,1,0:T(8,128)(2,1)} copy(bf16[2,512,128]{2,1,0:T(8,128)(2,1)} %get-tuple-element.12) | data formatting | bytes 524288
  95.9 4.5 %copy.15 = bf16[2,8192,128]{2,1,0:T(8,128)(2,1)} copy(bf16[2,8192,128]{2,1,0:T(8,128)(2,1)} %get-tuple-element.13) | data formatting | bytes 8388608

commit v2 on v1

v2 whole, which is shorter than its diff:
```python
import math

import jax
import jax.numpy as jnp
import numpy as np
from jax import lax
from jax.experimental import pallas as pl
from jax.experimental.pallas import tpu as pltpu
from jax.sharding import PartitionSpec as P

D = 8192
HD = 128
KVH = 8
QH = 32
LEN = 384
TOK = 2 * LEN
HEADS = 4
NS = 16
NT = 8
ROWS = D // NS
QB = 128
NB = LEN // QB

rope_base = 1000000.0
dpo_beta = 0.1
learning_rate = 0.2
mix_alpha = 0.6
norm_eps = 1e-06

MESH = pl.DeviceIdType.MESH
BF = jnp.bfloat16
F32 = jnp.float32

OWN, LFT, RGT, ZED, OPP, ZLF, ZRG, ZOP = range(8)


def rope_constants():
    positions = np.arange(LEN, dtype=np.float32)
    index = np.arange(HD // 2, dtype=np.float32)
    frequency = (np.float32(rope_base) ** (np.float32(-2.0) * index / np.float32(HD))).astype(np.float32)
    angles = (positions[:, None] * frequency[None, :]).astype(np.float32)
    cosine, sine = np.cos(angles), np.sin(angles)
    wide_cos = np.concatenate([cosine, cosine], axis=1)
    wide_sin = np.concatenate([-sine, sine], axis=1)
    return np.stack([wide_cos, wide_sin]), np.stack([wide_cos.T[: HD // 2], sine.T])


def dot(a, b, contract=((1,), (0,))):
    return lax.dot_general(a, b, (contract, ((), ())), preferred_element_type=F32)


def kernel(
    hid, pw, rw, pq, rq, ro, lens, rope, rope_t,
    newp, newr, marg,
    normed, pfull, gfull, rwv, pqv, rqv, rov, ropev, ropetv,
    acc, keys, values, cot, probs, grad_t,
    partial, sib_send, sib_recv, stage, net_recv,
    score_buf, sq_tensor, sq_shard,
    hid_sem, load_sem,
    g1_send, g1_recv, s1_send, s1_recv,
    g2_send, g2_recv, s2_send, s2_recv,
    rs_sib_send, rs_sib_recv, rs_send, rs_recv,
    sc_send, sc_recv, qt_send, qt_recv, qs_send, qs_recv,
):
    s = lax.axis_index("shard")
    t = lax.axis_index("tensor")
    x, h, c = s // 4, (s // 2) % 2, s % 2

    def shard_of(xx, hh, cc):
        return lax.rem(xx, 4) * 4 + hh * 2 + cc

    left = (shard_of(x + 3, h, c), t)
    right = (shard_of(x + 1, h, c), t)
    zed = (shard_of(x, 1 - h, c), t)
    sib = (shard_of(x, h, 1 - c), t)

    pair = {
        OWN: (x, h),
        LFT: (x + 3, h),
        RGT: (x + 1, h),
        ZED: (x, 1 - h),
        OPP: (x + 2, h),
        ZLF: (x + 3, 1 - h),
        ZRG: (x + 1, 1 - h),
        ZOP: (x + 2, 1 - h),
    }

    def rows_of(pos, cc):
        return pl.ds(pl.multiple_of(shard_of(*pair[pos], cc) * ROWS, ROWS), ROWS)

    def pair_rows(pos):
        return pl.ds(pl.multiple_of(shard_of(*pair[pos], 0) * ROWS, 2 * ROWS), 2 * ROWS)

    def send(src, dst, send_sem, recv_sem, device):
        pltpu.make_async_remote_copy(
            src_ref=src, dst_ref=dst, send_sem=send_sem, recv_sem=recv_sem,
            device_id=device, device_id_type=MESH,
        ).start()

    def all_sent(amount, send_sem, recv_sem):
        pltpu.make_async_remote_copy(
            src_ref=amount, dst_ref=amount, send_sem=send_sem, recv_sem=recv_sem,
            device_id=sib, device_id_type=MESH,
        ).wait_send()

    def arrived(dst, recv_sem, send_sem, device):
        pltpu.make_async_remote_copy(
            src_ref=dst, dst_ref=dst, send_sem=send_sem, recv_sem=recv_sem,
            device_id=device, device_id_type=MESH,
        ).wait_recv()

    barrier = pltpu.get_barrier_semaphore()
    for device in (left, right, zed, sib):
        pl.semaphore_signal(barrier, inc=1, device_id=device, device_id_type=MESH)
    for r in range(1, NT):
        pl.semaphore_signal(barrier, inc=1, device_id=(s, lax.rem(t + r, NT)), device_id_type=MESH)

    def load_hidden(b):
        copy = pltpu.make_async_copy(hid.at[pl.ds(256 * b, 256)], normed.at[pl.ds(256 * b, 256)], hid_sem.at[b])
        copy.start()
        return copy

    def load(src, dst, i):
        copy = pltpu.make_async_copy(src, dst, load_sem.at[i])
        copy.start()
        return copy

    hid_copies = [load_hidden(0)]
    pl.semaphore_wait(barrier, 4 + NT - 1)

    class Gather:
        def __init__(self, buf, own, lead, send_sem, recv_sem, sib_send_sem, sib_recv_sem):
            self.buf, self.own, self.lead = buf, own, lead
            self.send_sem, self.recv_sem = send_sem, recv_sem
            self.sib_send_sem, self.sib_recv_sem = sib_send_sem, sib_recv_sem

        def block(self, pos, cc, k):
            return self.buf.at[k, rows_of(pos, cc), :]

        def to(self, src, dst_pos_here, k, arrive_as, device):
            send(src, self.block(dst_pos_here, c, k), self.send_sem.at[0], self.recv_sem.at[arrive_as, k], device)

        def to_sib(self, src, pos, k):
            send(src, self.block(pos, c, k), self.sib_send_sem.at[0], self.sib_recv_sem.at[pos, k], sib)

        def start(self, k):
            src = self.own(k)
            self.to(src, OWN, k, LFT, right)
            self.to(src, OWN, k, RGT, left)
            self.to(src, OWN, k, ZED, zed)
            self.to_sib(src, OWN, k)

        def start_both(self):
            f, g = self.lead, 1 - self.lead
            self.to(self.own(f), OWN, f, LFT, right)
            self.to(self.own(g), OWN, g, RGT, left)
            self.to(self.own(f), OWN, f, ZED, zed)
            self.to(self.own(g), OWN, g, LFT, right)
            self.to(self.own(f), OWN, f, RGT, left)
            self.to(self.own(g), OWN, g, ZED, zed)
            self.to_sib(self.own(f), OWN, f)
            self.to_sib(self.own(g), OWN, g)

        def take(self, pos, k):
            lead = k == self.lead
            device = {LFT: left, RGT: right, ZED: zed, OPP: left if lead else right, ZLF: left, ZRG: right, ZOP: zed}[pos]
            arrived(self.block(pos, c, k), self.recv_sem.at[pos, k], self.send_sem.at[0], device)
            src = self.block(pos, c, k)
            if pos == LFT and lead:
                self.to(src, pos, k, OPP, right)
            if pos == RGT and not lead:
                self.to(src, pos, k, OPP, left)
            if pos == ZED:
                self.to(src, pos, k, ZLF, right)
                self.to(src, pos, k, ZRG, left)
            if pos == OPP:
                self.to(src, pos, k, ZOP, zed)
            self.to_sib(src, pos, k)

        def from_sib(self, pos, k):
            arrived(self.block(pos, 1 - c, k), self.sib_recv_sem.at[pos, k], self.sib_send_sem.at[0], sib)

        def finish(self):
            all_sent(self.buf.at[:, pl.ds(0, 7 * ROWS), :], self.send_sem.at[0], self.recv_sem.at[LFT, 0])
            all_sent(self.buf.at[:, pl.ds(0, 8 * ROWS), :], self.sib_send_sem.at[0], self.sib_recv_sem.at[OWN, 0])

    g1 = Gather(pfull, lambda k: pw.at[k], 0, g1_send, g1_recv, s1_send, s1_recv)
    g1.start_both()

    hid_copies += [load_hidden(1), load_hidden(2)]
    own_rows = rows_of(OWN, c)
    loads = [
        load(rw, rwv, 0),
        load(rq, rqv, 1),
        load(ro, rov, 2),
        load(rope, ropev, 3),
        load(pw, pfull.at[:, own_rows, :], 4),
        load(pq, pqv, 5),
        load(rope_t, ropetv, 6),
    ]

    def normalise(b):
        hid_copies[b].wait()

        @pl.loop(0, 8)
        def _(i):
            rows = pl.ds(pl.multiple_of(256 * b + i * 32, 32), 32)
            total = jnp.zeros((32, 512), F32)
            for j in range(D // 512):
                part = normed[rows, pl.ds(512 * j, 512)].astype(F32)
                total = total + part * part
            inverse = lax.rsqrt(jnp.sum(total, axis=-1, keepdims=True) * (1.0 / D) + norm_eps)
            for j in range(D // 512):
                cols = pl.ds(512 * j, 512)
                normed[rows, cols] = (normed[rows, cols].astype(F32) * inverse).astype(BF)

    def project(weights, cols, first):
        both = jnp.concatenate([weights[0, cols, :], weights[1, cols, :]], axis=1)
        product = dot(normed[:, cols], both)
        acc[...] = product if first else acc[...] + product

    def project_reference(first, last):
        if first == 0:
            project(rwv, pl.ds(0, 1024), True)
            first = 1

        @pl.loop(first, last)
        def _(j):
            project(rwv, pl.ds(pl.multiple_of(j * 1024, 1024), 1024), False)

    def heads_out():
        for q in range(2):
            rows = pl.ds(LEN * q, LEN)
            raw = acc[rows, 0:HD] * (D ** -0.5)
            turned = raw * ropev[0] + pltpu.roll(raw, HD // 2, 1) * ropev[1]
            keys[rows, :] = turned.astype(BF)
            values[rows, :] = (acc[rows, HD:] * (D ** -0.5)).astype(BF)

    def stacked(ref, q, b):
        rows = pl.ds(LEN * q + QB * b, QB)
        return jnp.concatenate([ref[rows, pl.ds(HD * g, HD)] for g in range(HEADS)], axis=0)

    def attend(q, b, queries, keep):
        n = QB * (b + 1)
        live = lens[q]
        seen = pl.ds(LEN * q, n)
        logits = dot(stacked(queries, q, b), keys[seen, :], ((1,), (1,))) * (math.log2(math.e) / math.sqrt(HD))
        key_at = lax.broadcasted_iota(jnp.int32, (1, n), 1)
        logits = logits + jnp.where(key_at < live, 0.0, -1e30)
        at = lax.broadcasted_iota(jnp.int32, (QB, QB), 0)
        after = lax.broadcasted_iota(jnp.int32, (QB, QB), 1) > at
        corner = jnp.where(after, -1e30, 0.0)
        corner = jnp.concatenate([corner] * HEADS, axis=0)
        if b == 0:
            logits = logits + corner
        else:
            logits = jnp.concatenate([logits[:, : n - QB], logits[:, n - QB :] + corner], axis=1)
        exponent = jnp.exp2(logits - jnp.max(logits, axis=-1, keepdims=True))
        probability = exponent * (1.0 / jnp.sum(exponent, axis=-1, keepdims=True))
        if keep:
            probs[q, b, :, 0:n] = probability
        attended = dot(probability.astype(BF), values[seen, :]).astype(BF).astype(F32)
        product = attended * stacked(rov, q, b).astype(F32)
        real = QB * b + lax.rem(lax.broadcasted_iota(jnp.int32, product.shape, 0), QB) < live
        product = jnp.where(real, product, 0.0)
        return jnp.sum(product.reshape(HEADS * QB // 8, 8, HD), axis=0)

    def scores(queries, keep):
        chosen = jnp.zeros((8, HD), F32)
        rejected = jnp.zeros((8, HD), F32)
        for b in range(NB):
            chosen = chosen + attend(0, b, queries, keep)
            rejected = rejected + attend(1, b, queries, keep)
        return chosen - rejected

    for b in range(3):
        normalise(b)
    for pos, k in ((LFT, 0), (RGT, 1), (ZED, 0)):
        g1.take(pos, k)
    loads[0].wait()
    project_reference(0, 5)
    for pos, k in ((ZED, 1), (LFT, 1), (RGT, 0)):
        g1.take(pos, k)
    project_reference(5, 8)
    for i in (1, 2, 3):
        loads[i].wait()
    heads_out()
    g1.take(OPP, 0)
    g1.take(OPP, 1)
    score_buf[t] = -scores(rqv, False)

    def project_policy(pos, first=False):
        for k in range(2):
            g1.from_sib(pos, k)
        project(pfull, pair_rows(pos), first)

    for i in (4, 5, 6):
        loads[i].wait()
    project_policy(OWN, True)
    g1.take(ZLF, 0)
    g1.take(ZRG, 0)
    for pos in (LFT, RGT, ZED):
        project_policy(pos)
    g1.take(ZOP, 0)
    g1.take(ZLF, 1)
    g1.take(ZRG, 1)
    project_policy(OPP)
    project_policy(ZLF)
    g1.take(ZOP, 1)
    project_policy(ZRG)
    project_policy(ZOP)

    heads_out()
    score_buf[t] = score_buf[t] + scores(pqv, True)
    for r in range(1, NT):
        send(score_buf.at[t], score_buf.at[t], sc_send.at[0], sc_recv.at[0], (s, lax.rem(t + r, NT)))

    def out_cotangent(q, b):
        out_cot = stacked(rov, q, b).astype(F32) * ((-1.0 if q == 0 else 1.0) / math.sqrt(QH * HD))
        real = QB * b + lax.rem(lax.broadcasted_iota(jnp.int32, out_cot.shape, 0), QB) < lens[q]
        return jnp.where(real, out_cot, 0.0).astype(BF)

    def pull_value(q, b):
        n = QB * (b + 1)
        seen = pl.ds(LEN * q, n)
        value_t = dot(out_cotangent(q, b), probs[q, b, :, 0:n].astype(BF), ((0,), (0,)))
        if b == NB - 1:
            grad_t[1, :, seen] = value_t
        else:
            grad_t[1, :, seen] += value_t

    def pull_key(q, b):
        n = QB * (b + 1)
        seen = pl.ds(LEN * q, n)
        probability = probs[q, b, :, 0:n]
        prob_cot = dot(out_cotangent(q, b), values[seen, :], ((1,), (1,))).astype(BF).astype(F32)
        weighted = probability * prob_cot
        logit_cot = weighted - probability * jnp.sum(weighted, axis=-1, keepdims=True)
        key_t = dot(stacked(pqv, q, b), logit_cot.astype(BF), ((0,), (0,)))
        if b == NB - 1:
            grad_t[0, :, seen] = key_t
        else:
            grad_t[0, :, seen] += key_t

    def value_cotangent():
        for q in range(2):
            for b in reversed(range(NB)):
                pull_value(q, b)
        cot[HD:, :] = grad_t[1].astype(BF)

    def key_cotangent(q):
        for b in reversed(range(NB)):
            pull_key(q, b)
        tokens = pl.ds(LEN * q, LEN)
        key_grad = (grad_t[0, :, tokens] * (1.0 / math.sqrt(HD))).astype(BF).astype(F32)
        upper, lower = key_grad[: HD // 2], key_grad[HD // 2 :]
        cosine, sine = ropetv[0], ropetv[1]
        cot[0 : HD // 2, tokens] = (upper * cosine + lower * sine).astype(BF)
        cot[HD // 2 : HD, tokens] = (lower * cosine - upper * sine).astype(BF)

    value_cotangent()
    key_cotangent(0)

    arrived(score_buf.at[pl.ds(0, NT - 1)], sc_recv.at[0], sc_send.at[0], (s, lax.rem(t + 1, NT)))
    score_total = score_buf[0]
    for r in range(1, NT):
        score_total = score_total + score_buf[r]
    score_total = jnp.sum(jnp.sum(score_total, axis=1, keepdims=True), axis=0, keepdims=True)
    margin = score_total * (dpo_beta / math.sqrt(QH * HD))
    marg[...] = jnp.broadcast_to(margin, (8, HD))
    weight = 1.0 / (1.0 + jnp.exp(margin))

    def product_of(pos, cc, k):
        out = dot(cot[pl.ds(HD * k, HD), :], normed[:, rows_of(pos, cc)]) * weight
        return out.T

    order = (ZOP, ZRG, ZLF, OPP, ZED, RGT, LFT, OWN)

    def push(i, k, slot, device):
        send(stage.at[i, k], net_recv.at[slot, k], rs_send.at[0], rs_recv.at[slot, k], device)

    def pull_net(slot, k, device):
        arrived(net_recv.at[slot, k], rs_recv.at[slot, k], rs_send.at[0], device)
        return net_recv[slot, k].astype(F32)

    SLOT_Z1, SLOT_R2L, SLOT_R2R, SLOT_3, SLOT_Z4, SLOT_5L, SLOT_5R = range(7)

    def compute_sib(i, k):
        sib_send[i, k] = product_of(order[i], 1 - c, k).astype(BF)
        send(sib_send.at[i, k], sib_recv.at[i, k], rs_sib_send.at[0], rs_sib_recv.at[i, k], sib)

    def compute_own(i, k):
        partial[i, k] = product_of(order[i], c, k)

    def compute(i, k):
        compute_sib(i, k)
        compute_own(i, k)

    def total_of(i, k, terms):
        arrived(sib_recv.at[i, k], rs_sib_recv.at[i, k], rs_sib_send.at[0], sib)
        total = partial[i, k] + sib_recv[i, k].astype(F32)
        for term in terms:
            total = total + term
        return total

    def put(i, k, slot, device, *terms):
        stage[i, k] = total_of(i, k, terms).astype(BF)
        push(i, k, slot, device)

    f, g = 1, 0
    for i in range(3):
        compute_sib(i, f)
    compute_own(0, f)
    put(0, f, SLOT_Z1, zed)
    compute_own(1, f)
    put(1, f, SLOT_R2L, right)
    compute_own(2, f)
    put(2, f, SLOT_R2R, left)
    key_cotangent(1)
    for i in range(3):
        compute_sib(i, g)
    compute_own(0, g)
    put(0, g, SLOT_Z1, zed)
    compute_own(1, g)
    put(1, g, SLOT_R2L, right)
    compute_own(2, g)
    put(2, g, SLOT_R2R, left)
    compute(3, f)
    compute(6, f)
    put(3, f, SLOT_3, right, pull_net(SLOT_Z1, f, zed))
    compute(4, f)
    put(6, f, SLOT_5R, left)
    compute(3, g)
    put(4, f, SLOT_Z4, zed, pull_net(SLOT_R2L, f, left), pull_net(SLOT_R2R, f, right))
    compute(5, g)
    put(3, g, SLOT_3, left, pull_net(SLOT_Z1, g, zed))
    compute(4, g)
    put(5, g, SLOT_5L, right)
    compute(5, f)
    put(4, g, SLOT_Z4, zed, pull_net(SLOT_R2L, g, left), pull_net(SLOT_R2R, g, right))
    compute(6, g)
    compute(7, f)
    compute(7, g)
    put(5, f, SLOT_5L, right, pull_net(SLOT_3, f, left))
    put(6, g, SLOT_5R, left, pull_net(SLOT_3, g, right))

    g2 = Gather(gfull, lambda k: gfull.at[k, own_rows, :], f, g2_send, g2_recv, s2_send, s2_recv)
    for k in (f, g):
        total = total_of(7, k, (
            pull_net(SLOT_Z4, k, zed), pull_net(SLOT_5L, k, left), pull_net(SLOT_5R, k, right),
        ))
        gfull[k, own_rows, :] = total.astype(BF)
        g2.start(k)
        sq_tensor[t, k] = jnp.sum((total * total).reshape(ROWS // 8, 8, HD), axis=0)

    for r in range(1, NT):
        send(sq_tensor.at[t], sq_tensor.at[t], qt_send.at[0], qt_recv.at[0], (s, lax.rem(t + r, NT)))
    for pos in (LFT, RGT, ZED):
        g2.take(pos, f)
    arrived(sq_tensor.at[pl.ds(0, NT - 1)], qt_recv.at[0], qt_send.at[0], (s, lax.rem(t + 1, NT)))
    squares = sq_tensor[0]
    for r in range(1, NT):
        squares = squares + sq_tensor[r]
    sq_shard[s] = squares
    for r in range(1, NS):
        send(sq_shard.at[s], sq_shard.at[s], qs_send.at[0], qs_recv.at[0], (lax.rem(s + r, NS), t))
    for pos in (ZED, LFT, RGT):
        g2.take(pos, g)
    g2.take(OPP, f)
    g2.take(OPP, g)
    g2.take(ZLF, f)
    g2.take(ZRG, f)
    arrived(sq_shard.at[pl.ds(0, NS - 1)], qs_recv.at[0], qs_send.at[0], (lax.rem(s + 1, NS), t))
    squares = sq_shard[0]
    for r in range(1, NS):
        squares = squares + sq_shard[r]
    step = []
    for k in range(2):
        mean = jnp.sum(jnp.sum(squares[k], axis=1, keepdims=True), axis=0, keepdims=True) * (1.0 / (D * KVH * HD))
        step.append(learning_rate * lax.rsqrt(mean + norm_eps))

    def update(pos, cc, k):
        rows = rows_of(pos, cc)
        fresh = (pfull[k, rows, :].astype(F32) - step[k] * gfull[k, rows, :].astype(F32)).astype(BF)
        newr[k, rows, :] = (mix_alpha * fresh.astype(F32) + (1.0 - mix_alpha) * rwv[k, rows, :].astype(F32)).astype(BF)
        return fresh

    def settle(pos, k):
        update(pos, c, k)
        g2.from_sib(pos, k)
        update(pos, 1 - c, k)

    for k in (f, g):
        newp[k] = update(OWN, c, k)
        g2.from_sib(OWN, k)
        update(OWN, 1 - c, k)
    for pos in (LFT, RGT, ZED):
        settle(pos, f)
    g2.take(ZOP, f)
    g2.take(ZLF, g)
    g2.take(ZRG, g)
    for pos in (LFT, RGT, ZED):
        settle(pos, g)
    settle(OPP, f)
    g2.take(ZOP, g)
    settle(OPP, g)
    for k in (f, g):
        settle(ZLF, k)
        settle(ZRG, k)
    settle(ZOP, f)
    settle(ZOP, g)

    g1.finish()
    g2.finish()
    all_sent(score_buf.at[pl.ds(0, NT - 1)], sc_send.at[0], sc_recv.at[0])
    all_sent(sq_tensor.at[pl.ds(0, NT - 1)], qt_send.at[0], qt_recv.at[0])
    all_sent(sq_shard.at[pl.ds(0, NS - 1)], qs_send.at[0], qs_recv.at[0])
    all_sent(sib_send, rs_sib_send.at[0], rs_sib_recv.at[0, 0])
    all_sent(stage.at[pl.ds(0, 7)], rs_send.at[0], rs_recv.at[0, 0])


def write_out(new_rows, new_reference, margin, rows_out, reference_out, margin_out, sem):
    copies = [
        pltpu.make_async_copy(new_reference, reference_out, sem.at[0]),
        pltpu.make_async_copy(new_rows, rows_out, sem.at[1]),
    ]
    for copy in copies:
        copy.start()
    margin_out[0] = margin[0, 0]
    for copy in copies:
        copy.wait()


def body(hidden_in, policy_weights, reference_weights, policy_queries, reference_queries, readout, lengths):
    rope, rope_t = rope_constants()
    anywhere = pl.BlockSpec(memory_space=pl.ANY)
    vmem = pl.BlockSpec(memory_space=pltpu.VMEM)
    dma = pltpu.SemaphoreType.DMA
    block = (2, ROWS, HD)
    new_rows, new_reference, margins = pl.pallas_call(
        kernel,
        out_shape=(
            pltpu.VMEM(block, BF),
            pltpu.VMEM((2, D, HD), BF),
            pltpu.VMEM((8, HD), F32),
        ),
        in_specs=[anywhere] * 6 + [pl.BlockSpec(memory_space=pltpu.SMEM)] + [anywhere] * 2,
        out_specs=(vmem, vmem, vmem),
        scratch_shapes=[
            pltpu.VMEM((TOK, D), BF),
            pltpu.VMEM((2, D, HD), BF),
            pltpu.VMEM((2, D, HD), BF),
            pltpu.VMEM((2, D, HD), BF),
            pltpu.VMEM((TOK, HEADS * HD), BF),
            pltpu.VMEM((TOK, HEADS * HD), BF),
            pltpu.VMEM((TOK, HEADS * HD), BF),
            pltpu.VMEM((2, LEN, HD), F32),
            pltpu.VMEM((2, HD // 2, LEN), F32),
            pltpu.VMEM((TOK, 2 * HD), F32),
            pltpu.VMEM((TOK, HD), BF),
            pltpu.VMEM((TOK, HD), BF),
            pltpu.VMEM((2 * HD, TOK), BF),
            pltpu.VMEM((2, NB, HEADS * QB, LEN), F32),
            pltpu.VMEM((2, HD, TOK), F32),
            pltpu.VMEM((8, *block), F32),
            pltpu.VMEM((8, *block), BF),
            pltpu.VMEM((8, *block), BF),
            pltpu.VMEM((8, *block), BF),
            pltpu.VMEM((7, *block), BF),
            pltpu.VMEM((NT, 8, HD), F32),
            pltpu.VMEM((NT, 2, 8, HD), F32),
            pltpu.VMEM((NS, 2, 8, HD), F32),
            dma((3,)), dma((7,)),
            dma((1,)), dma((8, 2)), dma((1,)), dma((8, 2)),
            dma((1,)), dma((8, 2)), dma((1,)), dma((8, 2)),
            dma((1,)), dma((8, 2)), dma((1,)), dma((7, 2)),
            dma((1,)), dma((1,)), dma((1,)), dma((1,)), dma((1,)), dma((1,)),
        ],
        compiler_params=pltpu.CompilerParams(
            collective_id=0, has_side_effects=True, vmem_limit_bytes=54 * 1024 * 1024
        ),
        cost_estimate=pl.CostEstimate(flops=12_000_000_000, bytes_accessed=24_000_000, transcendentals=2_000_000),
    )(
        hidden_in, policy_weights, reference_weights, policy_queries, reference_queries, readout, lengths,
        jnp.asarray(rope), jnp.asarray(rope_t),
    )
    return pl.pallas_call(
        write_out,
        out_shape=(
            jax.ShapeDtypeStruct(block, BF),
            jax.ShapeDtypeStruct((2, D, HD), BF),
            jax.ShapeDtypeStruct((1,), F32),
        ),
        in_specs=[vmem] * 3,
        out_specs=(anywhere, anywhere, pl.BlockSpec(memory_space=pltpu.SMEM)),
        scratch_shapes=[dma((2,))],
        compiler_params=pltpu.CompilerParams(vmem_limit_bytes=1024 * 1024),
    )(*(pltpu.with_memory_space_constraint(a, pltpu.VMEM) for a in (new_rows, new_reference, margins)))


def solution(mesh):
    return jax.shard_map(
        body,
        mesh=mesh,
        in_specs=(
            P("shard", None),
            P(None, "shard", "tensor"),
            P(None, None, "tensor"),
            P("shard", "tensor"),
            P("shard", "tensor"),
            P("shard", "tensor"),
            P("shard"),
        ),
        out_specs=(P(None, "shard", "tensor"), P(None, None, "tensor"), P("shard")),
        check_vma=False,
    )
```

time: 101 us -> 86.3 us (0.85)
  local copies, waits for them, and re-layouts: 7.33 us -> 0 us
  Pallas kernels: 92.4 us -> 85.4 us
    pallas_call x1 -> x2, Pallas kernels: 92.4 us -> 85.4 us  [the longest x1 82.7 us: body(): pl.pallas_call(kernel, out_shape=(pltpu.VMEM(block, BF), pltpu.VMEM((2, D...]
    unnamed x2 -> x0, local copies, waits for them, and re-layouts: 6.14 us -> none
    slice x1 -> x0, local copies, waits for them, and re-layouts: 1.19 us -> none  [body(): return (new_rows, new_reference, margins[0, :1])]
where the time goes in v2:
time: 86.3 us; the launch traced here: 86.2 us
  Pallas kernels  85.4 us (99%)
    pallas_call x1, Pallas kernels, body(): pl.pallas_call(kernel, out_shape=(pltpu.VMEM(block, BF), pltpu.VMEM((2, D...  82.7 us
    pallas_call x1, Pallas kernels, body(): pl.pallas_call(write_out, out_shape=(jax.ShapeDtypeStruct(block, BF), jax...  2.62 us

profile of v2, /device:TPU:1, one launch (start us, length us, event | category | flops | bytes accessed | tf_op | source)
XLA Modules:
  0.0 86.2 jit_solution(8030322727142565394)
XLA Ops:
  0.6 82.7 %shard_map.112 = (bf16[2,512,128]{2,1,0:T(8,128)(2,1)S(1)}, bf16[2,8192,128]{2,1,0:T(8,128)(2,1)S(1)}, f32[8,128]{1,0:T(8,128)S(1)}) custom-call(bf16[768,8192]{1,0:T(8,128)(2,1)} %hid.1, bf16[2,512,128]{2,1,0:T(8,128)(2,1)} %pw.1, bf16[2,8192,128]{2,1,0:T(8,128)(2,1)} %rw.1, bf16[768,512]{1,0:T(8,128)(2,1)} %pq.1, bf16[768,512]{1,0:T(8,128)(2,1)} %rq.1, ...), custom_call_target="tpu_custom_call" | custom-call | flops 12000000000 | bytes 24000000 | tf_op jit(solution)/shard_map/pallas_call | solution.py:540
  83.4 2.6 %shard_map.113 = (bf16[2,512,128]{2,1,0:T(8,128)(2,1)}, bf16[2,8192,128]{2,1,0:T(8,128)(2,1)}, f32[1]{0:T(128)}) custom-call(bf16[2,512,128]{2,1,0:T(8,128)(2,1)S(1)} %get-tuple-element.6.new_rows, bf16[2,8192,128]{2,1,0:T(8,128)(2,1)S(1)} %get-tuple-element.7.new_reference, f32[8,128]{1,0:T(8,128)S(1)} %get-tuple-element.8.margin), custom_call_target="tpu_custom_call" | custom-call | tf_op jit(solution)/shard_map/pallas_call | solution.py:587

commit v3 on v2

--- a/solution.py
+++ b/solution.py
@@ -32,6 +32,43 @@
 F32 = jnp.float32
 
 OWN, LFT, RGT, ZED, OPP, ZLF, ZRG, ZOP = range(8)
+PLACE = {"OWN": OWN, "L": LFT, "R": RGT, "Z": ZED, "O": OPP, "ZL": ZLF, "ZR": ZRG, "ZO": ZOP}
+HALF = ROWS // 2
+
+PLAN = (
+    ("co", 0, 0), ("cs", 2, 0), ("key",), ("cs", 0, 0), ("cs", 5, 1), ("cs", 2, 1), ("co", 1, 1), ("cs", 1, 1),
+    ("co", 5, 1), ("co", 6, 1), ("co", 2, 0), ("co", 0, 1), ("co", 2, 1), ("cs", 0, 1), ("put", 0, 1),
+    ("x", "R1", 1), ("put", 0, 0), ("x", "R1", 0), ("put", 5, 3), ("x", "R5r", 3), ("put", 2, 1), ("x", "R2l", 1),
+    ("co", 5, 0), ("put", 2, 2), ("x", "R2l", 2), ("put", 1, 2), ("x", "R2r", 2), ("put", 1, 3), ("co", 6, 0),
+    ("cs", 4, 0), ("put", 2, 0), ("put", 2, 3), ("cs", 7, 0), ("x", "R2r", 3), ("x", "R2l", 3), ("cs", 1, 0),
+    ("put", 0, 3), ("put", 0, 2), ("x", "R1", 2), ("co", 4, 1), ("co", 7, 1), ("cs", 3, 1), ("x", "R1", 3),
+    ("cs", 6, 0), ("co", 3, 0), ("x", "R2l", 0), ("cs", 3, 0), ("cs", 4, 1), ("cs", 6, 1), ("co", 1, 0),
+    ("put", 1, 0), ("x", "R2r", 0), ("put", 1, 1), ("co", 7, 0), ("x", "R2r", 1), ("cs", 7, 1), ("co", 3, 1),
+    ("cs", 5, 0), ("put", 6, 0), ("co", 4, 0), ("put", 3, 1), ("x", "R3", 1), ("put", 3, 0), ("put", 4, 2),
+    ("x", "R4", 2), ("x", "R5l", 0), ("put", 6, 2), ("put", 4, 3), ("x", "R4", 3), ("put", 3, 2), ("x", "R3", 2),
+    ("put", 5, 1), ("x", "R3", 0), ("put", 4, 0), ("x", "R4", 0), ("put", 3, 3), ("x", "R3", 3), ("x", "R5r", 1),
+    ("put", 4, 1), ("x", "R4", 1), ("put", 6, 1), ("x", "R5l", 1), ("x", "R5l", 2), ("put", 5, 2), ("x", "R5r", 2),
+    ("put", 5, 0), ("x", "R5r", 0), ("put", 6, 3), ("x", "R5l", 3), ("put", 7, 1), ("x", "ownz", 1),
+    ("x", "own+", 1), ("x", "own-", 1), ("put", 7, 2), ("x", "ownz", 2), ("x", "own+", 2), ("x", "own-", 2),
+    ("put", 7, 0), ("x", "own+", 0), ("put", 7, 3), ("x", "ownz", 3), ("x", "own-", 3), ("qt",), ("x", "ownz", 0),
+    ("x", "own+", 3), ("t", "R", 1), ("x", "fO", 1), ("t", "L", 1), ("t", "Z", 1), ("x", "z-", 1), ("t", "R", 2),
+    ("t", "L", 2), ("x", "fO", 2), ("t", "Z", 2), ("t", "L", 0), ("x", "fO", 0), ("t", "R", 3), ("x", "fO", 3),
+    ("qsum",), ("t", "Z", 3), ("x", "z+", 3), ("x", "z-", 3), ("t", "O", 1), ("x", "zz", 1), ("t", "L", 3),
+    ("t", "Z", 0), ("x", "z+", 0), ("x", "z-", 0), ("t", "O", 2), ("x", "zz", 2), ("t", "ZR", 1), ("x", "z+", 1),
+    ("x", "z-", 2), ("t", "O", 3), ("x", "zz", 3), ("t", "O", 0), ("x", "zz", 0), ("x", "z+", 2), ("x", "own-", 0),
+    ("t", "ZL", 3), ("t", "ZR", 3), ("t", "ZO", 1), ("step",), ("u", "ZO", 1), ("u", "L", 0), ("u", "ZR", 3),
+    ("us", "R", 3), ("us", "Z", 1), ("us", "ZR", 1), ("u", "O", 2), ("u", "O", 3), ("u", "OWN", 2),
+    ("us", "OWN", 2), ("u", "OWN", 0), ("u", "R", 3), ("u", "Z", 0), ("u", "L", 1), ("t", "ZR", 0), ("us", "ZL", 3),
+    ("u", "ZR", 0), ("us", "ZR", 3), ("us", "L", 2), ("us", "ZO", 1), ("us", "R", 1), ("us", "OWN", 0),
+    ("us", "O", 3), ("u", "L", 3), ("u", "ZL", 3), ("u", "Z", 2), ("us", "O", 1), ("us", "Z", 0), ("u", "OWN", 3),
+    ("u", "L", 2), ("us", "R", 2), ("u", "O", 0), ("us", "L", 1), ("u", "Z", 3), ("t", "ZL", 1), ("u", "ZL", 1),
+    ("us", "ZR", 0), ("t", "ZR", 2), ("u", "ZR", 2), ("t", "ZL", 2), ("t", "R", 0), ("u", "R", 0), ("t", "ZO", 0),
+    ("u", "ZL", 2), ("t", "ZL", 0), ("t", "ZO", 3), ("u", "ZO", 3), ("us", "OWN", 1), ("us", "O", 2),
+    ("us", "Z", 2), ("t", "ZO", 2), ("u", "ZO", 2), ("us", "OWN", 3), ("u", "Z", 1), ("us", "Z", 3),
+    ("us", "ZL", 1), ("us", "L", 0), ("u", "ZO", 0), ("us", "ZR", 2), ("u", "ZL", 0), ("us", "ZL", 2),
+    ("u", "O", 1), ("us", "R", 0), ("u", "R", 1), ("us", "ZO", 0), ("us", "ZL", 0), ("us", "O", 0), ("us", "ZO", 3),
+    ("u", "ZR", 1), ("u", "R", 2), ("u", "OWN", 1), ("us", "ZO", 2), ("us", "L", 3),
+)
 
 
 def rope_constants():
@@ -375,15 +412,36 @@
         return out.T
 
     order = (ZOP, ZRG, ZLF, OPP, ZED, RGT, LFT, OWN)
-
-    def push(i, k, slot, device):
-        send(stage.at[i, k], net_recv.at[slot, k], rs_send.at[0], rs_recv.at[slot, k], device)
-
-    def pull_net(slot, k, device):
-        arrived(net_recv.at[slot, k], rs_recv.at[slot, k], rs_send.at[0], device)
-        return net_recv[slot, k].astype(F32)
-
     SLOT_Z1, SLOT_R2L, SLOT_R2R, SLOT_3, SLOT_Z4, SLOT_5L, SLOT_5R = range(7)
+
+    def kind(q):
+        return 1 - q // 2
+
+    def turns_right(q):
+        return q % 2 == 0
+
+    def part(q):
+        return pl.ds(HALF * (q % 2), HALF)
+
+    def piece(pos, cc, q):
+        return pl.ds(pl.multiple_of(shard_of(*pair[pos], cc) * ROWS + HALF * (q % 2), HALF), HALF)
+
+    def grad_piece(pos, cc, q):
+        return gfull.at[kind(q), piece(pos, cc, q), :]
+
+    def push(i, q, slot, device):
+        src, dst = stage.at[i, kind(q), part(q)], net_recv.at[slot, kind(q), part(q)]
+        send(src, dst, rs_send.at[0], rs_recv.at[slot, q], device)
+
+    def pull_net(slot, q, device):
+        arrived(net_recv.at[slot, kind(q), part(q)], rs_recv.at[slot, q], rs_send.at[0], device)
+        return net_recv[slot, kind(q), part(q)].astype(F32)
+
+    def spread(pos, q, arrive_as, device):
+        send(grad_piece(pos, c, q), grad_piece(pos, c, q), g2_send.at[0], g2_recv.at[arrive_as, q], device)
+
+    def spread_sib(pos, q):
+        send(grad_piece(pos, c, q), grad_piece(pos, c, q), s2_send.at[0], s2_recv.at[pos, q], sib)
 
     def compute_sib(i, k):
         sib_send[i, k] = product_of(order[i], 1 - c, k).astype(BF)
@@ -392,126 +450,134 @@
     def compute_own(i, k):
         partial[i, k] = product_of(order[i], c, k)
 
-    def compute(i, k):
-        compute_sib(i, k)
-        compute_own(i, k)
-
-    def total_of(i, k, terms):
-        arrived(sib_recv.at[i, k], rs_sib_recv.at[i, k], rs_sib_send.at[0], sib)
-        total = partial[i, k] + sib_recv[i, k].astype(F32)
-        for term in terms:
-            total = total + term
-        return total
-
-    def put(i, k, slot, device, *terms):
-        stage[i, k] = total_of(i, k, terms).astype(BF)
-        push(i, k, slot, device)
-
-    f, g = 1, 0
-    for i in range(3):
-        compute_sib(i, f)
-    compute_own(0, f)
-    put(0, f, SLOT_Z1, zed)
-    compute_own(1, f)
-    put(1, f, SLOT_R2L, right)
-    compute_own(2, f)
-    put(2, f, SLOT_R2R, left)
-    key_cotangent(1)
-    for i in range(3):
-        compute_sib(i, g)
-    compute_own(0, g)
-    put(0, g, SLOT_Z1, zed)
-    compute_own(1, g)
-    put(1, g, SLOT_R2L, right)
-    compute_own(2, g)
-    put(2, g, SLOT_R2R, left)
-    compute(3, f)
-    compute(6, f)
-    put(3, f, SLOT_3, right, pull_net(SLOT_Z1, f, zed))
-    compute(4, f)
-    put(6, f, SLOT_5R, left)
-    compute(3, g)
-    put(4, f, SLOT_Z4, zed, pull_net(SLOT_R2L, f, left), pull_net(SLOT_R2R, f, right))
-    compute(5, g)
-    put(3, g, SLOT_3, left, pull_net(SLOT_Z1, g, zed))
-    compute(4, g)
-    put(5, g, SLOT_5L, right)
-    compute(5, f)
-    put(4, g, SLOT_Z4, zed, pull_net(SLOT_R2L, g, left), pull_net(SLOT_R2R, g, right))
-    compute(6, g)
-    compute(7, f)
-    compute(7, g)
-    put(5, f, SLOT_5L, right, pull_net(SLOT_3, f, left))
-    put(6, g, SLOT_5R, left, pull_net(SLOT_3, g, right))
-
-    g2 = Gather(gfull, lambda k: gfull.at[k, own_rows, :], f, g2_send, g2_recv, s2_send, s2_recv)
-    for k in (f, g):
-        total = total_of(7, k, (
-            pull_net(SLOT_Z4, k, zed), pull_net(SLOT_5L, k, left), pull_net(SLOT_5R, k, right),
-        ))
-        gfull[k, own_rows, :] = total.astype(BF)
-        g2.start(k)
-        sq_tensor[t, k] = jnp.sum((total * total).reshape(ROWS // 8, 8, HD), axis=0)
-
-    for r in range(1, NT):
-        send(sq_tensor.at[t], sq_tensor.at[t], qt_send.at[0], qt_recv.at[0], (s, lax.rem(t + r, NT)))
-    for pos in (LFT, RGT, ZED):
-        g2.take(pos, f)
-    arrived(sq_tensor.at[pl.ds(0, NT - 1)], qt_recv.at[0], qt_send.at[0], (s, lax.rem(t + 1, NT)))
-    squares = sq_tensor[0]
-    for r in range(1, NT):
-        squares = squares + sq_tensor[r]
-    sq_shard[s] = squares
-    for r in range(1, NS):
-        send(sq_shard.at[s], sq_shard.at[s], qs_send.at[0], qs_recv.at[0], (lax.rem(s + r, NS), t))
-    for pos in (ZED, LFT, RGT):
-        g2.take(pos, g)
-    g2.take(OPP, f)
-    g2.take(OPP, g)
-    g2.take(ZLF, f)
-    g2.take(ZRG, f)
-    arrived(sq_shard.at[pl.ds(0, NS - 1)], qs_recv.at[0], qs_send.at[0], (lax.rem(s + 1, NS), t))
-    squares = sq_shard[0]
-    for r in range(1, NS):
-        squares = squares + sq_shard[r]
+    def start(name, q):
+        if name == "R1":
+            push(0, q, SLOT_Z1, zed)
+        elif name == "R2r":
+            push(1, q, SLOT_R2L, right)
+        elif name == "R2l":
+            push(2, q, SLOT_R2R, left)
+        elif name == "R3":
+            push(3, q, SLOT_3, right if turns_right(q) else left)
+        elif name == "R4":
+            push(4, q, SLOT_Z4, zed)
+        elif name == "R5r":
+            push(5, q, SLOT_5L, right)
+        elif name == "R5l":
+            push(6, q, SLOT_5R, left)
+        elif name == "own+":
+            spread(OWN, q, LFT, right)
+        elif name == "own-":
+            spread(OWN, q, RGT, left)
+        elif name == "ownz":
+            spread(OWN, q, ZED, zed)
+        elif name == "fO" and turns_right(q):
+            spread(LFT, q, OPP, right)
+        elif name == "fO":
+            spread(RGT, q, OPP, left)
+        elif name == "zz":
+            spread(OPP, q, ZOP, zed)
+        elif name == "z+":
+            spread(ZED, q, ZLF, right)
+        elif name == "z-":
+            spread(ZED, q, ZRG, left)
+        else:
+            raise ValueError(name)
+
+    from_core = set()
+    summed = set()
+
+    def put(i, q):
+        k = kind(q)
+        if (i, k) not in from_core:
+            from_core.add((i, k))
+            arrived(sib_recv.at[i, k], rs_sib_recv.at[i, k], rs_sib_send.at[0], sib)
+        total = partial[i, k, part(q)] + sib_recv[i, k, part(q)].astype(F32)
+        if i == 3:
+            total = total + pull_net(SLOT_Z1, q, zed)
+        elif i == 4:
+            total = total + pull_net(SLOT_R2L, q, left) + pull_net(SLOT_R2R, q, right)
+        elif i == 5 and turns_right(q):
+            total = total + pull_net(SLOT_3, q, left)
+        elif i == 6 and not turns_right(q):
+            total = total + pull_net(SLOT_3, q, right)
+        if i < 7:
+            stage[i, k, part(q)] = total.astype(BF)
+            return
+        total = total + pull_net(SLOT_Z4, q, zed)
+        total = total + pull_net(SLOT_5L, q, left)
+        total = total + pull_net(SLOT_5R, q, right)
+        gfull[k, piece(OWN, c, q), :] = total.astype(BF)
+        spread_sib(OWN, q)
+        squares = jnp.sum((total * total).reshape(HALF // 8, 8, HD), axis=0)
+        sq_tensor[t, k] = sq_tensor[t, k] + squares if k in summed else squares
+        summed.add(k)
+
+    def take(pos, q):
+        device = {
+            LFT: left, RGT: right, ZED: zed, OPP: left if turns_right(q) else right, ZLF: left, ZRG: right, ZOP: zed,
+        }[pos]
+        arrived(grad_piece(pos, c, q), g2_recv.at[pos, q], g2_send.at[0], device)
+        spread_sib(pos, q)
+
+    def send_squares():
+        for r in range(1, NT):
+            send(sq_tensor.at[t], sq_tensor.at[t], qt_send.at[0], qt_recv.at[0], (s, lax.rem(t + r, NT)))
+
+    def add_squares():
+        arrived(sq_tensor.at[pl.ds(0, NT - 1)], qt_recv.at[0], qt_send.at[0], (s, lax.rem(t + 1, NT)))
+        squares = sq_tensor[0]
+        for r in range(1, NT):
+            squares = squares + sq_tensor[r]
+        sq_shard[s] = squares
+        for r in range(1, NS):
+            send(sq_shard.at[s], sq_shard.at[s], qs_send.at[0], qs_recv.at[0], (lax.rem(s + r, NS), t))
+
     step = []
-    for k in range(2):
-        mean = jnp.sum(jnp.sum(squares[k], axis=1, keepdims=True), axis=0, keepdims=True) * (1.0 / (D * KVH * HD))
-        step.append(learning_rate * lax.rsqrt(mean + norm_eps))
-
-    def update(pos, cc, k):
-        rows = rows_of(pos, cc)
+
+    def find_step():
+        arrived(sq_shard.at[pl.ds(0, NS - 1)], qs_recv.at[0], qs_send.at[0], (lax.rem(s + 1, NS), t))
+        squares = sq_shard[0]
+        for r in range(1, NS):
+            squares = squares + sq_shard[r]
+        for k in range(2):
+            mean = jnp.sum(jnp.sum(squares[k], axis=1, keepdims=True), axis=0, keepdims=True) * (1.0 / (D * KVH * HD))
+            step.append(learning_rate * lax.rsqrt(mean + norm_eps))
+
+    def update(pos, cc, q):
+        k, rows = kind(q), piece(pos, cc, q)
         fresh = (pfull[k, rows, :].astype(F32) - step[k] * gfull[k, rows, :].astype(F32)).astype(BF)
         newr[k, rows, :] = (mix_alpha * fresh.astype(F32) + (1.0 - mix_alpha) * rwv[k, rows, :].astype(F32)).astype(BF)
         return fresh
 
-    def settle(pos, k):
-        update(pos, c, k)
-        g2.from_sib(pos, k)
-        update(pos, 1 - c, k)
-
-    for k in (f, g):
-        newp[k] = update(OWN, c, k)
-        g2.from_sib(OWN, k)
-        update(OWN, 1 - c, k)
-    for pos in (LFT, RGT, ZED):
-        settle(pos, f)
-    g2.take(ZOP, f)
-    g2.take(ZLF, g)
-    g2.take(ZRG, g)
-    for pos in (LFT, RGT, ZED):
-        settle(pos, g)
-    settle(OPP, f)
-    g2.take(ZOP, g)
-    settle(OPP, g)
-    for k in (f, g):
-        settle(ZLF, k)
-        settle(ZRG, k)
-    settle(ZOP, f)
-    settle(ZOP, g)
+    def update_own_core(pos, q):
+        fresh = update(pos, c, q)
+        if pos == OWN:
+            newp[kind(q), part(q), :] = fresh
+
+    def update_other_core(pos, q):
+        arrived(grad_piece(pos, 1 - c, q), s2_recv.at[pos, q], s2_send.at[0], sib)
+        update(pos, 1 - c, q)
+
+    act = {
+        "key": lambda: key_cotangent(1),
+        "cs": lambda i, first: compute_sib(i, 1 - first),
+        "co": lambda i, first: compute_own(i, 1 - first),
+        "put": put,
+        "x": start,
+        "t": lambda pos, q: take(PLACE[pos], q),
+        "qt": send_squares,
+        "qsum": add_squares,
+        "step": find_step,
+        "u": lambda pos, q: update_own_core(PLACE[pos], q),
+        "us": lambda pos, q: update_other_core(PLACE[pos], q),
+    }
+    for name, *rest in PLAN:
+        act[name](*rest)
 
     g1.finish()
-    g2.finish()
+    all_sent(gfull.at[:, pl.ds(0, 7 * ROWS), :], g2_send.at[0], g2_recv.at[LFT, 0])
+    all_sent(gfull.at[:, pl.ds(0, 8 * ROWS), :], s2_send.at[0], s2_recv.at[OWN, 0])
     all_sent(score_buf.at[pl.ds(0, NT - 1)], sc_send.at[0], sc_recv.at[0])
     all_sent(sq_tensor.at[pl.ds(0, NT - 1)], qt_send.at[0], qt_recv.at[0])
     all_sent(sq_shard.at[pl.ds(0, NS - 1)], qs_send.at[0], qs_recv.at[0])
@@ -572,8 +638,8 @@
             pltpu.VMEM((NS, 2, 8, HD), F32),
             dma((3,)), dma((7,)),
             dma((1,)), dma((8, 2)), dma((1,)), dma((8, 2)),
-            dma((1,)), dma((8, 2)), dma((1,)), dma((8, 2)),
-            dma((1,)), dma((8, 2)), dma((1,)), dma((7, 2)),
+            dma((1,)), dma((8, 4)), dma((1,)), dma((8, 4)),
+            dma((1,)), dma((8, 2)), dma((1,)), dma((7, 4)),
             dma((1,)), dma((1,)), dma((1,)), dma((1,)), dma((1,)), dma((1,)),
         ],
         compiler_params=pltpu.CompilerParams(

time: 86.3 us -> 81.9 us (0.949)
  Pallas kernels: 85.4 us -> 81 us
    pallas_call x1, Pallas kernels: 82.7 us -> 78.4 us  [body(): pl.pallas_call(kernel, out_shape=(pltpu.VMEM(block, BF), pltpu.VMEM((2, D...]
where the time goes in v3:
time: 81.9 us; the launch traced here: 81.8 us
  Pallas kernels  81 us (99%)
    pallas_call x1, Pallas kernels, body(): pl.pallas_call(kernel, out_shape=(pltpu.VMEM(block, BF), pltpu.VMEM((2, D...  78.4 us
    pallas_call x1, Pallas kernels, body(): pl.pallas_call(write_out, out_shape=(jax.ShapeDtypeStruct(block, BF), jax...  2.62 us

profile of v3, /device:TPU:1, one launch (start us, length us, event | category | flops | bytes accessed | tf_op | source)
XLA Modules:
  0.0 81.8 jit_solution(12465038893623288714)
XLA Ops:
  0.6 78.4 %shard_map.112 = (bf16[2,512,128]{2,1,0:T(8,128)(2,1)S(1)}, bf16[2,8192,128]{2,1,0:T(8,128)(2,1)S(1)}, f32[8,128]{1,0:T(8,128)S(1)}) custom-call(bf16[768,8192]{1,0:T(8,128)(2,1)} %hid.1, bf16[2,512,128]{2,1,0:T(8,128)(2,1)} %pw.1, bf16[2,8192,128]{2,1,0:T(8,128)(2,1)} %rw.1, bf16[768,512]{1,0:T(8,128)(2,1)} %pq.1, bf16[768,512]{1,0:T(8,128)(2,1)} %rq.1, ...), custom_call_target="tpu_custom_call" | custom-call | flops 12000000000 | bytes 24000000 | tf_op jit(solution)/shard_map/pallas_call | solution.py:606
  79.0 2.6 %shard_map.113 = (bf16[2,512,128]{2,1,0:T(8,128)(2,1)}, bf16[2,8192,128]{2,1,0:T(8,128)(2,1)}, f32[1]{0:T(128)}) custom-call(bf16[2,512,128]{2,1,0:T(8,128)(2,1)S(1)} %get-tuple-element.6.new_rows, bf16[2,8192,128]{2,1,0:T(8,128)(2,1)S(1)} %get-tuple-element.7.new_reference, f32[8,128]{1,0:T(8,128)S(1)} %get-tuple-element.8.margin), custom_call_target="tpu_custom_call" | custom-call | tf_op jit(solution)/shard_map/pallas_call | solution.py:653

commit v4 on v3

--- a/solution.py
+++ b/solution.py
@@ -36,38 +36,38 @@
 HALF = ROWS // 2
 
 PLAN = (
-    ("co", 0, 0), ("cs", 2, 0), ("key",), ("cs", 0, 0), ("cs", 5, 1), ("cs", 2, 1), ("co", 1, 1), ("cs", 1, 1),
-    ("co", 5, 1), ("co", 6, 1), ("co", 2, 0), ("co", 0, 1), ("co", 2, 1), ("cs", 0, 1), ("put", 0, 1),
-    ("x", "R1", 1), ("put", 0, 0), ("x", "R1", 0), ("put", 5, 3), ("x", "R5r", 3), ("put", 2, 1), ("x", "R2l", 1),
-    ("co", 5, 0), ("put", 2, 2), ("x", "R2l", 2), ("put", 1, 2), ("x", "R2r", 2), ("put", 1, 3), ("co", 6, 0),
-    ("cs", 4, 0), ("put", 2, 0), ("put", 2, 3), ("cs", 7, 0), ("x", "R2r", 3), ("x", "R2l", 3), ("cs", 1, 0),
-    ("put", 0, 3), ("put", 0, 2), ("x", "R1", 2), ("co", 4, 1), ("co", 7, 1), ("cs", 3, 1), ("x", "R1", 3),
-    ("cs", 6, 0), ("co", 3, 0), ("x", "R2l", 0), ("cs", 3, 0), ("cs", 4, 1), ("cs", 6, 1), ("co", 1, 0),
-    ("put", 1, 0), ("x", "R2r", 0), ("put", 1, 1), ("co", 7, 0), ("x", "R2r", 1), ("cs", 7, 1), ("co", 3, 1),
-    ("cs", 5, 0), ("put", 6, 0), ("co", 4, 0), ("put", 3, 1), ("x", "R3", 1), ("put", 3, 0), ("put", 4, 2),
-    ("x", "R4", 2), ("x", "R5l", 0), ("put", 6, 2), ("put", 4, 3), ("x", "R4", 3), ("put", 3, 2), ("x", "R3", 2),
-    ("put", 5, 1), ("x", "R3", 0), ("put", 4, 0), ("x", "R4", 0), ("put", 3, 3), ("x", "R3", 3), ("x", "R5r", 1),
-    ("put", 4, 1), ("x", "R4", 1), ("put", 6, 1), ("x", "R5l", 1), ("x", "R5l", 2), ("put", 5, 2), ("x", "R5r", 2),
-    ("put", 5, 0), ("x", "R5r", 0), ("put", 6, 3), ("x", "R5l", 3), ("put", 7, 1), ("x", "ownz", 1),
-    ("x", "own+", 1), ("x", "own-", 1), ("put", 7, 2), ("x", "ownz", 2), ("x", "own+", 2), ("x", "own-", 2),
-    ("put", 7, 0), ("x", "own+", 0), ("put", 7, 3), ("x", "ownz", 3), ("x", "own-", 3), ("qt",), ("x", "ownz", 0),
-    ("x", "own+", 3), ("t", "R", 1), ("x", "fO", 1), ("t", "L", 1), ("t", "Z", 1), ("x", "z-", 1), ("t", "R", 2),
-    ("t", "L", 2), ("x", "fO", 2), ("t", "Z", 2), ("t", "L", 0), ("x", "fO", 0), ("t", "R", 3), ("x", "fO", 3),
-    ("qsum",), ("t", "Z", 3), ("x", "z+", 3), ("x", "z-", 3), ("t", "O", 1), ("x", "zz", 1), ("t", "L", 3),
-    ("t", "Z", 0), ("x", "z+", 0), ("x", "z-", 0), ("t", "O", 2), ("x", "zz", 2), ("t", "ZR", 1), ("x", "z+", 1),
-    ("x", "z-", 2), ("t", "O", 3), ("x", "zz", 3), ("t", "O", 0), ("x", "zz", 0), ("x", "z+", 2), ("x", "own-", 0),
-    ("t", "ZL", 3), ("t", "ZR", 3), ("t", "ZO", 1), ("step",), ("u", "ZO", 1), ("u", "L", 0), ("u", "ZR", 3),
-    ("us", "R", 3), ("us", "Z", 1), ("us", "ZR", 1), ("u", "O", 2), ("u", "O", 3), ("u", "OWN", 2),
-    ("us", "OWN", 2), ("u", "OWN", 0), ("u", "R", 3), ("u", "Z", 0), ("u", "L", 1), ("t", "ZR", 0), ("us", "ZL", 3),
-    ("u", "ZR", 0), ("us", "ZR", 3), ("us", "L", 2), ("us", "ZO", 1), ("us", "R", 1), ("us", "OWN", 0),
-    ("us", "O", 3), ("u", "L", 3), ("u", "ZL", 3), ("u", "Z", 2), ("us", "O", 1), ("us", "Z", 0), ("u", "OWN", 3),
-    ("u", "L", 2), ("us", "R", 2), ("u", "O", 0), ("us", "L", 1), ("u", "Z", 3), ("t", "ZL", 1), ("u", "ZL", 1),
-    ("us", "ZR", 0), ("t", "ZR", 2), ("u", "ZR", 2), ("t", "ZL", 2), ("t", "R", 0), ("u", "R", 0), ("t", "ZO", 0),
-    ("u", "ZL", 2), ("t", "ZL", 0), ("t", "ZO", 3), ("u", "ZO", 3), ("us", "OWN", 1), ("us", "O", 2),
-    ("us", "Z", 2), ("t", "ZO", 2), ("u", "ZO", 2), ("us", "OWN", 3), ("u", "Z", 1), ("us", "Z", 3),
-    ("us", "ZL", 1), ("us", "L", 0), ("u", "ZO", 0), ("us", "ZR", 2), ("u", "ZL", 0), ("us", "ZL", 2),
-    ("u", "O", 1), ("us", "R", 0), ("u", "R", 1), ("us", "ZO", 0), ("us", "ZL", 0), ("us", "O", 0), ("us", "ZO", 3),
-    ("u", "ZR", 1), ("u", "R", 2), ("u", "OWN", 1), ("us", "ZO", 2), ("us", "L", 3),
+    ("cs", 0, 0), ("co", 0, 0), ("cs", 2, 0), ("cs", 1, 0), ("co", 1, 0), ("co", 2, 0), ("key",), ("cs", 1, 1),
+    ("cs", 0, 1), ("put", 0, 0), ("x", "R1", 0), ("put", 1, 1), ("x", "R2r", 1), ("put", 1, 0), ("x", "R2r", 0),
+    ("put", 2, 0), ("x", "R2l", 0), ("co", 0, 1), ("put", 2, 1), ("x", "R2l", 1), ("cs", 2, 1), ("cs", 5, 1),
+    ("cs", 3, 1), ("put", 0, 1), ("x", "R1", 1), ("co", 3, 1), ("cs", 4, 0), ("put", 0, 3), ("x", "R1", 3),
+    ("co", 5, 0), ("co", 2, 1), ("cs", 3, 0), ("co", 1, 1), ("put", 1, 3), ("x", "R2r", 3), ("put", 2, 2),
+    ("x", "R2l", 2), ("put", 2, 3), ("x", "R2l", 3), ("put", 0, 2), ("x", "R1", 2), ("put", 1, 2), ("x", "R2r", 2),
+    ("co", 6, 0), ("co", 5, 1), ("co", 7, 1), ("cs", 6, 0), ("co", 6, 1), ("co", 7, 0), ("co", 3, 0), ("put", 3, 0),
+    ("x", "R3", 0), ("cs", 6, 1), ("co", 4, 0), ("put", 4, 1), ("x", "R4", 1), ("put", 3, 1), ("x", "R3", 1),
+    ("put", 4, 0), ("x", "R4", 0), ("co", 4, 1), ("put", 5, 3), ("x", "R5r", 3), ("cs", 5, 0), ("put", 6, 0),
+    ("cs", 4, 1), ("cs", 7, 0), ("put", 3, 3), ("x", "R3", 3), ("cs", 7, 1), ("x", "R5l", 0), ("put", 6, 2),
+    ("put", 3, 2), ("x", "R3", 2), ("put", 5, 1), ("x", "R5r", 1), ("put", 4, 3), ("x", "R4", 3), ("put", 4, 2),
+    ("x", "R4", 2), ("put", 5, 0), ("put", 6, 1), ("x", "R5l", 1), ("x", "R5r", 0), ("put", 6, 3), ("x", "R5l", 3),
+    ("x", "R5l", 2), ("put", 5, 2), ("x", "R5r", 2), ("put", 7, 1), ("x", "ownz", 1), ("x", "own+", 1),
+    ("x", "own-", 1), ("put", 7, 0), ("x", "ownz", 0), ("x", "own+", 0), ("put", 7, 3), ("x", "own-", 3),
+    ("x", "ownz", 3), ("x", "own-", 0), ("put", 7, 2), ("x", "own+", 2), ("x", "ownz", 2), ("qt",), ("t", "L", 1),
+    ("t", "R", 1), ("x", "fO", 1), ("t", "Z", 1), ("x", "z+", 1), ("t", "L", 0), ("x", "fO", 0), ("t", "R", 3),
+    ("x", "fO", 3), ("t", "Z", 0), ("t", "L", 2), ("x", "fO", 2), ("t", "R", 0), ("t", "Z", 3), ("x", "z-", 3),
+    ("qsum",), ("x", "z-", 1), ("t", "ZL", 1), ("t", "O", 1), ("x", "zz", 1), ("t", "Z", 2), ("x", "z+", 2),
+    ("x", "z+", 3), ("x", "own-", 2), ("t", "O", 0), ("x", "zz", 0), ("t", "O", 3), ("x", "z+", 0), ("x", "z-", 0),
+    ("t", "O", 2), ("x", "zz", 2), ("t", "ZR", 3), ("x", "zz", 3), ("x", "own+", 3), ("x", "z-", 2), ("t", "ZL", 2),
+    ("t", "ZR", 1), ("t", "ZO", 1), ("step",), ("us", "Z", 0), ("u", "OWN", 0), ("u", "L", 0), ("us", "ZR", 3),
+    ("us", "Z", 2), ("u", "R", 0), ("u", "Z", 3), ("u", "R", 1), ("t", "R", 2), ("u", "O", 3), ("u", "R", 2),
+    ("u", "Z", 0), ("us", "L", 2), ("us", "ZL", 2), ("us", "R", 0), ("us", "ZR", 1), ("u", "OWN", 3),
+    ("t", "ZL", 3), ("u", "R", 3), ("us", "O", 0), ("u", "ZR", 3), ("t", "ZL", 0), ("t", "ZR", 0), ("u", "ZR", 0),
+    ("u", "ZL", 0), ("us", "L", 1), ("us", "Z", 3), ("u", "Z", 2), ("us", "R", 2), ("us", "ZO", 1), ("t", "ZO", 2),
+    ("u", "ZO", 2), ("u", "ZL", 1), ("t", "ZO", 0), ("t", "L", 3), ("u", "ZO", 0), ("us", "ZL", 3), ("t", "ZO", 3),
+    ("t", "ZR", 2), ("us", "ZL", 0), ("u", "ZO", 3), ("us", "ZR", 0), ("u", "ZR", 2), ("u", "ZO", 1),
+    ("us", "ZL", 1), ("u", "L", 2), ("u", "ZL", 3), ("us", "OWN", 0), ("u", "OWN", 2), ("us", "ZO", 2),
+    ("us", "O", 2), ("u", "O", 2), ("us", "L", 0), ("us", "ZO", 0), ("us", "L", 3), ("us", "R", 3), ("u", "ZR", 1),
+    ("u", "ZL", 2), ("u", "O", 0), ("us", "ZR", 2), ("us", "O", 1), ("us", "ZO", 3), ("u", "Z", 1), ("us", "R", 1),
+    ("u", "O", 1), ("u", "OWN", 1), ("us", "OWN", 1), ("u", "L", 1), ("us", "OWN", 2), ("u", "L", 3),
+    ("us", "O", 3), ("us", "OWN", 3), ("us", "Z", 1),
 )
 
 
@@ -310,20 +310,21 @@
             rejected = rejected + attend(1, b, queries, keep)
         return chosen - rejected
 
-    for b in range(3):
-        normalise(b)
+    normalise(0)
+    normalise(1)
     for pos, k in ((LFT, 0), (RGT, 1), (ZED, 0)):
         g1.take(pos, k)
+    normalise(2)
     loads[0].wait()
-    project_reference(0, 5)
+    project_reference(0, 3)
     for pos, k in ((ZED, 1), (LFT, 1), (RGT, 0)):
         g1.take(pos, k)
-    project_reference(5, 8)
+    project_reference(3, 8)
+    g1.take(OPP, 0)
+    g1.take(OPP, 1)
     for i in (1, 2, 3):
         loads[i].wait()
     heads_out()
-    g1.take(OPP, 0)
-    g1.take(OPP, 1)
     score_buf[t] = -scores(rqv, False)
 
     def project_policy(pos, first=False):
@@ -398,6 +399,23 @@
     value_cotangent()
     key_cotangent(0)
 
+    order = (ZOP, ZRG, ZLF, OPP, ZED, RGT, LFT, OWN)
+
+    def product_of(pos, cc, k):
+        return dot(cot[pl.ds(HD * k, HD), :], normed[:, rows_of(pos, cc)]).T
+
+    for i in range(2):
+        acc[0:ROWS, pl.ds(HD * i, HD)] = product_of(order[i], 1 - c, 1)
+    last = product_of(order[2], 1 - c, 1)
+    acc[ROWS:, 0:HD] = last[:HALF]
+    acc[ROWS:, HD:] = last[HALF:]
+    partial[0, 1] = product_of(order[0], c, 1)
+
+    def ready_product(i):
+        if i < 2:
+            return acc[0:ROWS, pl.ds(HD * i, HD)]
+        return jnp.concatenate([acc[ROWS:, 0:HD], acc[ROWS:, HD:]], axis=0)
+
     arrived(score_buf.at[pl.ds(0, NT - 1)], sc_recv.at[0], sc_send.at[0], (s, lax.rem(t + 1, NT)))
     score_total = score_buf[0]
     for r in range(1, NT):
@@ -407,11 +425,6 @@
     marg[...] = jnp.broadcast_to(margin, (8, HD))
     weight = 1.0 / (1.0 + jnp.exp(margin))
 
-    def product_of(pos, cc, k):
-        out = dot(cot[pl.ds(HD * k, HD), :], normed[:, rows_of(pos, cc)]) * weight
-        return out.T
-
-    order = (ZOP, ZRG, ZLF, OPP, ZED, RGT, LFT, OWN)
     SLOT_Z1, SLOT_R2L, SLOT_R2R, SLOT_3, SLOT_Z4, SLOT_5L, SLOT_5R = range(7)
 
     def kind(q):
@@ -444,10 +457,13 @@
         send(grad_piece(pos, c, q), grad_piece(pos, c, q), s2_send.at[0], s2_recv.at[pos, q], sib)
 
     def compute_sib(i, k):
-        sib_send[i, k] = product_of(order[i], 1 - c, k).astype(BF)
+        product = ready_product(i) if i < 3 and k == 1 else product_of(order[i], 1 - c, k)
+        sib_send[i, k] = (product * weight).astype(BF)
         send(sib_send.at[i, k], sib_recv.at[i, k], rs_sib_send.at[0], rs_sib_recv.at[i, k], sib)
 
     def compute_own(i, k):
+        if (i, k) == (0, 1):
+            return
         partial[i, k] = product_of(order[i], c, k)
 
     def start(name, q):
@@ -492,7 +508,7 @@
         if (i, k) not in from_core:
             from_core.add((i, k))
             arrived(sib_recv.at[i, k], rs_sib_recv.at[i, k], rs_sib_send.at[0], sib)
-        total = partial[i, k, part(q)] + sib_recv[i, k, part(q)].astype(F32)
+        total = partial[i, k, part(q)] * weight + sib_recv[i, k, part(q)].astype(F32)
         if i == 3:
             total = total + pull_net(SLOT_Z1, q, zed)
         elif i == 4:

time: 81.9 us -> 80.6 us (0.984)
  Pallas kernels: 81 us -> 79.7 us
    pallas_call x1, Pallas kernels: 78.4 us -> 77 us  [body(): pl.pallas_call(kernel, out_shape=(pltpu.VMEM(block, BF), pltpu.VMEM((2, D...]
where the time goes in v4:
time: 80.6 us; the launch traced here: 80.5 us
  Pallas kernels  79.7 us (99%)
    pallas_call x1, Pallas kernels, body(): pl.pallas_call(kernel, out_shape=(pltpu.VMEM(block, BF), pltpu.VMEM((2, D...  77 us
    pallas_call x1, Pallas kernels, body(): pl.pallas_call(write_out, out_shape=(jax.ShapeDtypeStruct(block, BF), jax...  2.62 us

profile of v4, /device:TPU:1, one launch (start us, length us, event | category | flops | bytes accessed | tf_op | source)
XLA Modules:
  0.0 80.5 jit_solution(4139877398657103290)
XLA Ops:
  0.6 77.0 %shard_map.112 = (bf16[2,512,128]{2,1,0:T(8,128)(2,1)S(1)}, bf16[2,8192,128]{2,1,0:T(8,128)(2,1)S(1)}, f32[8,128]{1,0:T(8,128)S(1)}) custom-call(bf16[768,8192]{1,0:T(8,128)(2,1)} %hid.1, bf16[2,512,128]{2,1,0:T(8,128)(2,1)} %pw.1, bf16[2,8192,128]{2,1,0:T(8,128)(2,1)} %rw.1, bf16[768,512]{1,0:T(8,128)(2,1)} %pq.1, bf16[768,512]{1,0:T(8,128)(2,1)} %rq.1, ...), custom_call_target="tpu_custom_call" | custom-call | flops 12000000000 | bytes 24000000 | tf_op jit(solution)/shard_map/pallas_call | solution.py:622
  77.7 2.6 %shard_map.113 = (bf16[2,512,128]{2,1,0:T(8,128)(2,1)}, bf16[2,8192,128]{2,1,0:T(8,128)(2,1)}, f32[1]{0:T(128)}) custom-call(bf16[2,512,128]{2,1,0:T(8,128)(2,1)S(1)} %get-tuple-element.6.new_rows, bf16[2,8192,128]{2,1,0:T(8,128)(2,1)S(1)} %get-tuple-element.7.new_reference, f32[8,128]{1,0:T(8,128)S(1)} %get-tuple-element.8.margin), custom_call_target="tpu_custom_call" | custom-call | tf_op jit(solution)/shard_map/pallas_call | solution.py:669
